TPU v7x, 256 devices: a whole 4x4x8 slice. The times are simulated.
256 devices in a mesh: row: 32 (over y, x, core), col: 8 (over z).
Axes of the slice: x: 4, y: 4, z: 8, core: 2. Of those that a mesh axis runs over, the one named last changes fastest.
Arguments:
- probes: float32 [8, 2048, 2048], P(None, 'row', 'col'), may hold values from -6 to 6
- kappa_sq: float32 [2048, 2048], P('row', 'col'), may hold values from 0.05 to 1
- conduct: float32 [2048, 2048], P('row', 'col'), may hold values from 0.05 to 0.25
- inv_mass: float32 [2048, 2048], P('row', 'col'), may hold values from 0.5 to 2
- spai: bfloat16 [25, 2048, 2048], P(None, 'row', 'col'), may hold values from -0.04 to 2, as said below
- sea_mask: int32 [2048, 2048], P('row', 'col'), may hold values 0 or 1
Outputs:
- solution_field: float32 [8, 2048, 2048], P(None, 'row', 'col')
- residual: float32 [8, 2048, 2048], P(None, 'row', 'col')
Inputs may be any that keep to these rules, and one draw needn't show every extreme that they name: `spai`: channel 12 (no offset) lies in 1 to 2, every other channel in -0.04 to 0.04.
All inputs are finite; a program needn't handle non-finite values. No bound on the sum of `sea_mask` on one device may be relied on, other than what follows from the above.
Results may differ from a plain program's by a relative error of at most 0.0003.
Values may be sent and summed in bfloat16 or wider, within the bound.
A program may use at most 64 MiB of HBM per device.

v0:
```python
import jax
import jax.numpy as jnp
from jax import lax
from jax.sharding import PartitionSpec as P

ITERS = 2


def padded(block, sides, width):
    for axis, dim in sides:
        count = lax.axis_size(axis)
        forward = [(i, i + 1) for i in range(count - 1)]
        backward = [(target, source) for source, target in forward]
        low = lax.ppermute(
            lax.slice_in_dim(block, block.shape[dim] - width, None, axis=dim), axis, forward
        )
        high = lax.ppermute(lax.slice_in_dim(block, 0, width, axis=dim), axis, backward)
        block = jnp.concatenate([low, block, high], axis=dim)
    return block


def laplace(padded_field, kap, padded_cond):
    centre = padded_field[:, 1:-1, 1:-1]
    cond_centre = padded_cond[1:-1, 1:-1]
    total = kap * centre
    shifts = [
        (slice(0, -2), slice(1, -1)),
        (slice(2, None), slice(1, -1)),
        (slice(1, -1), slice(0, -2)),
        (slice(1, -1), slice(2, None)),
    ]
    for first, second in shifts:
        cond_near = padded_cond[first, second]
        field_near = padded_field[:, first, second]
        total = total + 0.5 * (cond_centre + cond_near) * (centre - field_near)
    return total


def symmetric(weights, padded_weights, nrow, ncol):
    rows_out = []
    for offset in range(25):
        shift_a = offset // 5 - 2
        shift_b = offset % 5 - 2
        mirror = padded_weights[
            24 - offset, 2 + shift_a : 2 + shift_a + nrow, 2 + shift_b : 2 + shift_b + ncol
        ]
        rows_out.append(0.5 * (weights[offset] + mirror))
    return jnp.stack(rows_out)


def combine(sym, padded_field, nrow, ncol):
    total = jnp.zeros((padded_field.shape[0], nrow, ncol), jnp.float32)
    for offset in range(25):
        shift_a = offset // 5 - 2
        shift_b = offset % 5 - 2
        total = (
            total
            + sym[offset][None]
            * padded_field[:, 2 + shift_a : 2 + shift_a + nrow, 2 + shift_b : 2 + shift_b + ncol]
        )
    return total


def gram(left, right):
    return jnp.einsum("kij,lij->kl", left, right, precision=lax.Precision.HIGHEST)


def mix(coef, field):
    return jnp.einsum("kl,kij->lij", coef, field, precision=lax.Precision.HIGHEST)


def solve_small(matrix, rhs):
    matrix = 0.5 * (matrix + matrix.T)
    factor = jnp.linalg.cholesky(matrix)
    return jax.scipy.linalg.cho_solve((factor, True), rhs)


def shards(probes, kappa_sq, conduct, inv_mass, spai, sea_mask):
    nrow, ncol = kappa_sq.shape
    sea = sea_mask.astype(jnp.float32)
    stacked = jnp.stack([kappa_sq, conduct, inv_mass, sea])
    coefs = padded(stacked, (("row", 1), ("col", 2)), 2)
    cond_one = coefs[1, 1:-1, 1:-1]
    weights = spai.astype(jnp.float32)
    weight_pad = padded(spai, (("row", 1), ("col", 2)), 2).astype(jnp.float32)
    sym = symmetric(weights, weight_pad, nrow, ncol)

    def precond(field):
        field_pad = padded(field, (("row", 1), ("col", 2)), 2)
        return combine(sym, field_pad, nrow, ncol)

    solution_field = jnp.zeros_like(probes)
    residual = probes
    zvec = precond(residual)
    direction = zvec
    gamma = lax.psum(gram(residual, zvec), ("row", "col"))
    for step in range(ITERS):
        masked = sea[None] * direction
        masked_pad = padded(masked, (("row", 1), ("col", 2)), 1)
        inner = laplace(masked_pad, kappa_sq, cond_one)
        scaled = inv_mass[None] * inner
        scaled_pad = padded(scaled, (("row", 1), ("col", 2)), 1)
        outer = laplace(scaled_pad, kappa_sq, cond_one)
        image = sea[None] * outer + (1.0 - sea[None]) * direction
        curv = lax.psum(gram(direction, image), ("row", "col"))
        alpha = solve_small(curv, gamma)
        solution_field = solution_field + mix(alpha, direction)
        residual = residual - mix(alpha, image)
        if step + 1 < ITERS:
            zvec = precond(residual)
            gamma_new = lax.psum(gram(residual, zvec), ("row", "col"))
            beta = solve_small(gamma, gamma_new)
            direction = zvec + mix(beta, direction)
            gamma = gamma_new
    return (solution_field, residual)


def solution(mesh):
    in_specs = (
        P(None, "row", "col"),
        P("row", "col"),
        P("row", "col"),
        P("row", "col"),
        P(None, "row", "col"),
        P("row", "col"),
    )
    out_specs = (P(None, "row", "col"), P(None, "row", "col"))
    return jax.shard_map(shards, mesh=mesh, in_specs=in_specs, out_specs=out_specs, check_vma=False)
```

profile of v0, /device:TPU:1, one launch (start us, length us, event | category | flops | bytes accessed | tf_op | source)
XLA Modules:
  0.0 430.1 jit_solution(2445809010060195622)
XLA Ops:
  1.7 4.5 %collective-permute-start = (bf16[25,2,256]{2,1,0:T(2,128)(2,1)S(1)}, bf16[25,2,256]{2,1,0:T(2,128)(2,1)S(1)}, u32[]{:S(2)}, u32[]{:S(2)}) collective-permute-start(bf16[25,2,256]{2,1,0:T(2,128)(2,1)S(1)} %get-tuple-element.36), channel_id=1, source_target_pairs={{0,8},{8,16},{16,24},{24,32},{32,40},{40,48},{48,56},{56,64},{64,7... | collective-permute-start | bytes 76808 | tf_op jit(solution)/shard_map/ppermute | solution.py:14
  9.8 3.6 collective-permute-start.8
  16.3 3.8 collective-permute-start.4
  23.7 3.5 collective-permute-start.10
  29.8 4.2 collective-permute-start.2
  35.4 4.2 collective-permute-start.6
  39.6 4.7 %collective-permute-done.2 = bf16[25,68,2]{2,1,0:T(8,128)(2,1)S(1)} collective-permute-done((bf16[25,68,2]{2,1,0:T(8,128)(2,1)S(1)}, bf16[25,68,2]{2,1,0:T(8,128)(2,1)S(1)}, u32[]{:S(2)}, u32[]{:S(2)}) %collective-permute-start.2) | collective-permute-done | bytes 6832 | tf_op jit(solution)/shard_map/ppermute | solution.py:14
  49.3 4.6 %collective-permute-done.7 = f32[8,68,2]{2,0,1:T(8,128)S(1)} collective-permute-done((f32[8,68,2]{2,0,1:T(8,128)S(1)}, f32[8,68,2]{2,0,1:T(8,128)S(1)}, u32[]{:S(2)}, u32[]{:S(2)}) %collective-permute-start.7) | collective-permute-done | bytes 4384 | tf_op jit(solution)/shard_map/ppermute | solution.py:17
  53.9 5.2 %broadcast_multiply_fusion.1 = (f32[8,64,256]{2,0,1:T(8,128)S(1)}, f32[8,64,256]{2,0,1:T(8,128)S(1)}) fusion(f32[64,256]{1,0:T(8,128)S(1)} %get-tuple-element.76, f32[8,68,2]{2,0,1:T(8,128)S(1)} %collective-permute-done.7, f32[8,68,256]{2,0,1:T(8,128)S(1)} %get-tuple-element.80, f32[64,256]{1,0:T(8,128)S(1)} %get-tuple-element.11, ...), kind=kLoop, calls=%fused_computation.269 | loop fusion | flops 9175040 | bytes 5939712 | tf_op jit(solution)/shard_map/mul | solution.py:98
  59.2 4.3 collective-permute-start.12
  68.7 4.6 %collective-permute-start.14 = (f32[8,66,1]{2,0,1:T(8,128)S(1)}, f32[8,66,1]{2,0,1:T(8,128)S(1)}, u32[]{:S(2)}, u32[]{:S(2)}) collective-permute-start(f32[8,66,1]{2,0,1:T(8,128)S(1)} %get-tuple-element.50), channel_id=1, source_target_pairs={{0,1},{1,2},{2,3},{3,4},{4,5},{5,6},{6,7},{8,9},{9,10},{10,11},{11... | collective-permute-start | bytes 6344 | tf_op jit(solution)/shard_map/ppermute | solution.py:14
  78.1 5.0 %collective-permute-done.15 = f32[8,66,1]{2,0,1:T(8,128)S(1)} collective-permute-done((f32[8,66,1]{2,0,1:T(8,128)S(1)}, f32[8,66,1]{2,0,1:T(8,128)S(1)}, u32[]{:S(2)}, u32[]{:S(2)}) %collective-permute-start.15) | collective-permute-done | bytes 2144 | tf_op jit(solution)/shard_map/ppermute | solution.py:17
  83.7 4.2 collective-permute-start.16
  93.1 4.9 %collective-permute-start.18 = (f32[8,66,1]{2,0,1:T(8,128)S(1)}, f32[8,66,1]{2,0,1:T(8,128)S(1)}, u32[]{:S(2)}, u32[]{:S(2)}) collective-permute-start(f32[8,66,1]{2,0,1:T(8,128)S(1)} %get-tuple-element.48), channel_id=1, source_target_pairs={{0,1},{1,2},{2,3},{3,4},{4,5},{5,6},{6,7},{8,9},{9,10},{10,11},{11... | collective-permute-start | bytes 6344 | tf_op jit(solution)/shard_map/ppermute | solution.py:14
  102.8 4.1 collective-permute-done.19
  108.7 82.6 %all-reduce = (f32[8,8]{1,0:T(8,128)S(1)}, f32[8,8]{1,0:T(8,128)S(1)}) all-reduce(f32[8,8]{1,0:T(8,128)S(1)} %convolution_bitcast_fusion.5, f32[8,8]{1,0:T(8,128)S(1)} %convolution_bitcast_fusion.6), channel_id=1, replica_groups=mesh['row'=32,'col'=8] {'row','col'}, use_global_device_ids=true, to_apply=%region_3.5 | all-reduce | flops 128 | bytes 1024 | tf_op jit(solution)/shard_map/psum | solution.py:96
  213.2 4.6 %collective-permute-done.23 = f32[8,68,2]{2,0,1:T(8,128)} collective-permute-done((f32[8,68,2]{2,0,1:T(8,128)S(1)}, f32[8,68,2]{2,0,1:T(8,128)}, u32[]{:S(2)}, u32[]{:S(2)}) %collective-permute-start.23) | collective-permute-done | bytes 4384 | tf_op jit(solution)/shard_map/ppermute | solution.py:17
  219.2 3.5 fusion.9
  224.1 76.3 %psum.30 = f32[8,8]{1,0:T(8,128)S(1)} all-reduce(f32[8,8]{1,0:T(8,128)S(1)} %convolution_bitcast_fusion.3), channel_id=1, replica_groups=mesh['row'=32,'col'=8] {'row','col'}, use_global_device_ids=true, to_apply=%region_4.7 | all-reduce | flops 64 | bytes 512 | tf_op jit(solution)/shard_map/psum | solution.py:111
  302.7 3.7 collective-permute-start.24
  318.1 4.3 collective-permute-done.27
  335.0 3.5 collective-permute-done.30
  338.5 4.8 %collective-permute-done.31 = f32[8,66,1]{2,0,1:T(8,128)S(1)} collective-permute-done((f32[8,66,1]{2,0,1:T(8,128)S(1)}, f32[8,66,1]{2,0,1:T(8,128)S(1)}, u32[]{:S(2)}, u32[]{:S(2)}) %collective-permute-start.31) | collective-permute-done | bytes 2144 | tf_op jit(solution)/shard_map/ppermute | solution.py:17
  345.1 78.2 %psum.31 = f32[8,8]{1,0:T(8,128)S(1)} all-reduce(f32[8,8]{1,0:T(8,128)S(1)} %convolution_bitcast_fusion.1), channel_id=1, replica_groups=mesh['row'=32,'col'=8] {'row','col'}, use_global_device_ids=true, to_apply=%region_5.8 | all-reduce | flops 64 | bytes 512 | tf_op jit(solution)/shard_map/psum | solution.py:105
  (199 shorter events, 101.4 us)
Async XLA Ops:
  1.7 27.2 %collective-permute-start = (bf16[25,2,256]{2,1,0:T(2,128)(2,1)S(1)}, bf16[25,2,256]{2,1,0:T(2,128)(2,1)S(1)}, u32[]{:S(2)}, u32[]{:S(2)}) collective-permute-start(bf16[25,2,256]{2,1,0:T(2,128)(2,1)S(1)} %get-tuple-element.36), channel_id=1, source_target_pairs={{0,8},{8,16},{16,24},{24,32},{32,40},{40,48},{48,56},{56,64},{64,7... | collective-permute-start | bytes 76808 | tf_op jit(solution)/shard_map/ppermute | solution.py:14
  6.2 22.7 %collective-permute-start.1 = (bf16[25,2,256]{2,1,0:T(2,128)(2,1)S(1)}, bf16[25,2,256]{2,1,0:T(2,128)(2,1)S(1)}, u32[]{:S(2)}, u32[]{:S(2)}) collective-permute-start(bf16[25,2,256]{2,1,0:T(2,128)(2,1)S(1)} %get-tuple-element.37), channel_id=1, source_target_pairs={{8,0},{16,8},{24,16},{32,24},{40,32},{48,40},{56,48},{64,56},{72,6... | collective-permute-start | bytes 76808 | tf_op jit(solution)/shard_map/ppermute | solution.py:17
  9.8 11.6 %collective-permute-start.8 = (f32[4,2,256]{2,1,0:T(2,128)S(1)}, f32[4,2,256]{2,1,0:T(2,128)S(1)}, u32[]{:S(2)}, u32[]{:S(2)}) collective-permute-start(f32[4,2,256]{2,1,0:T(2,128)S(1)} %get-tuple-element.69), channel_id=1, source_target_pairs={{0,8},{8,16},{16,24},{24,32},{32,40},{40,48},{48,56},{56,64},{64,7... | collective-permute-start | bytes 24584 | tf_op jit(solution)/shard_map/ppermute | solution.py:14
  13.4 10.1 %collective-permute-start.9 = (f32[4,2,256]{2,1,0:T(2,128)S(1)}, f32[4,2,256]{2,1,0:T(2,128)S(1)}, u32[]{:S(2)}, u32[]{:S(2)}) collective-permute-start(f32[4,2,256]{2,1,0:T(2,128)S(1)} %get-tuple-element.70), channel_id=1, source_target_pairs={{8,0},{16,8},{24,16},{32,24},{40,32},{48,40},{56,48},{64,56},{72,6... | collective-permute-start | bytes 24584 | tf_op jit(solution)/shard_map/ppermute | solution.py:17
  16.3 11.0 %collective-permute-start.4 = (f32[8,2,256]{2,0,1:T(8,128)S(1)}, f32[8,2,256]{2,0,1:T(8,128)S(1)}, u32[]{:S(2)}, u32[]{:S(2)}) collective-permute-start(f32[8,2,256]{2,0,1:T(8,128)S(1)} %copy.43), channel_id=1, source_target_pairs={{0,8},{8,16},{16,24},{24,32},{32,40},{40,48},{48,56},{56,64},{64,7... | collective-permute-start | bytes 49160 | tf_op jit(solution)/shard_map/ppermute | solution.py:14
  21.4 7.5 %collective-permute-start.5 = (f32[8,2,256]{2,0,1:T(8,128)S(1)}, f32[8,2,256]{2,0,1:T(8,128)S(1)}, u32[]{:S(2)}, u32[]{:S(2)}) collective-permute-start(f32[8,2,256]{2,0,1:T(8,128)S(1)} %copy.44), channel_id=1, source_target_pairs={{8,0},{16,8},{24,16},{32,24},{40,32},{48,40},{56,48},{64,56},{72,6... | collective-permute-start | bytes 49160 | tf_op jit(solution)/shard_map/ppermute | solution.py:17
  23.7 41.8 %collective-permute-start.10 = (f32[4,68,2]{2,1,0:T(8,128)S(1)}, f32[4,68,2]{2,1,0:T(8,128)S(1)}, u32[]{:S(2)}, u32[]{:S(2)}) collective-permute-start(f32[4,68,2]{2,1,0:T(8,128)S(1)} %get-tuple-element.67), channel_id=1, source_target_pairs={{0,1},{1,2},{2,3},{3,4},{4,5},{5,6},{6,7},{8,9},{9,10},{10,11},{11... | collective-permute-start | bytes 6536 | tf_op jit(solution)/shard_map/ppermute | solution.py:14
  27.3 38.2 %collective-permute-start.11 = (f32[4,68,2]{2,1,0:T(8,128)S(1)}, f32[4,68,2]{2,1,0:T(8,128)S(1)}, u32[]{:S(2)}, u32[]{:S(2)}) collective-permute-start(f32[4,68,2]{2,1,0:T(8,128)S(1)} %get-tuple-element.68), channel_id=1, source_target_pairs={{1,0},{2,1},{3,2},{4,3},{5,4},{6,5},{7,6},{9,8},{10,9},{11,10},{12... | collective-permute-start | bytes 6536 | tf_op jit(solution)/shard_map/ppermute | solution.py:17
  29.8 14.5 %collective-permute-start.2 = (bf16[25,68,2]{2,1,0:T(8,128)(2,1)S(1)}, bf16[25,68,2]{2,1,0:T(8,128)(2,1)S(1)}, u32[]{:S(2)}, u32[]{:S(2)}) collective-permute-start(bf16[25,68,2]{2,1,0:T(8,128)(2,1)S(1)} %get-tuple-element.34), channel_id=1, source_target_pairs={{0,1},{1,2},{2,3},{3,4},{4,5},{5,6},{6,7},{8,9},{9,10},{10,11},{11... | collective-permute-start | bytes 20408 | tf_op jit(solution)/shard_map/ppermute | solution.py:14
  34.0 13.4 %collective-permute-start.3 = (bf16[25,68,2]{2,1,0:T(8,128)(2,1)S(1)}, bf16[25,68,2]{2,1,0:T(8,128)(2,1)S(1)}, u32[]{:S(2)}, u32[]{:S(2)}) collective-permute-start(bf16[25,68,2]{2,1,0:T(8,128)(2,1)S(1)} %get-tuple-element.35), channel_id=1, source_target_pairs={{1,0},{2,1},{3,2},{4,3},{5,4},{6,5},{7,6},{9,8},{10,9},{11,10},{12... | collective-permute-start | bytes 20408 | tf_op jit(solution)/shard_map/ppermute | solution.py:17
  35.4 13.9 %collective-permute-start.6 = (f32[8,68,2]{2,0,1:T(8,128)S(1)}, f32[8,68,2]{2,0,1:T(8,128)S(1)}, u32[]{:S(2)}, u32[]{:S(2)}) collective-permute-start(f32[8,68,2]{2,0,1:T(8,128)S(1)} %get-tuple-element.42), channel_id=1, source_target_pairs={{0,1},{1,2},{2,3},{3,4},{4,5},{5,6},{6,7},{8,9},{9,10},{10,11},{11... | collective-permute-start | bytes 13064 | tf_op jit(solution)/shard_map/ppermute | solution.py:14
  44.3 9.6 %collective-permute-start.7 = (f32[8,68,2]{2,0,1:T(8,128)S(1)}, f32[8,68,2]{2,0,1:T(8,128)S(1)}, u32[]{:S(2)}, u32[]{:S(2)}) collective-permute-start(f32[8,68,2]{2,0,1:T(8,128)S(1)} %get-tuple-element.43), channel_id=1, source_target_pairs={{1,0},{2,1},{3,2},{4,3},{5,4},{6,5},{7,6},{9,8},{10,9},{11,10},{12... | collective-permute-start | bytes 13064 | tf_op jit(solution)/shard_map/ppermute | solution.py:17
  59.2 6.4 %collective-permute-start.12 = (f32[8,1,256]{2,0,1:T(8,128)S(1)}, f32[8,1,256]{2,0,1:T(8,128)S(1)}, u32[]{:S(2)}, u32[]{:S(2)}) collective-permute-start(f32[8,1,256]{2,0,1:T(8,128)S(1)} %get-tuple-element.60), channel_id=1, source_target_pairs={{0,8},{8,16},{16,24},{24,32},{32,40},{40,48},{48,56},{56,64},{64,7... | collective-permute-start | bytes 24584 | tf_op jit(solution)/shard_map/ppermute | solution.py:14
  68.7 9.4 %collective-permute-start.14 = (f32[8,66,1]{2,0,1:T(8,128)S(1)}, f32[8,66,1]{2,0,1:T(8,128)S(1)}, u32[]{:S(2)}, u32[]{:S(2)}) collective-permute-start(f32[8,66,1]{2,0,1:T(8,128)S(1)} %get-tuple-element.50), channel_id=1, source_target_pairs={{0,1},{1,2},{2,3},{3,4},{4,5},{5,6},{6,7},{8,9},{9,10},{10,11},{11... | collective-permute-start | bytes 6344 | tf_op jit(solution)/shard_map/ppermute | solution.py:14
  73.3 9.9 %collective-permute-start.15 = (f32[8,66,1]{2,0,1:T(8,128)S(1)}, f32[8,66,1]{2,0,1:T(8,128)S(1)}, u32[]{:S(2)}, u32[]{:S(2)}) collective-permute-start(f32[8,66,1]{2,0,1:T(8,128)S(1)} %get-tuple-element.51), channel_id=1, source_target_pairs={{1,0},{2,1},{3,2},{4,3},{5,4},{6,5},{7,6},{9,8},{10,9},{11,10},{12... | collective-permute-start | bytes 6344 | tf_op jit(solution)/shard_map/ppermute | solution.py:17
  83.7 6.2 %collective-permute-start.16 = (f32[8,1,256]{2,0,1:T(8,128)S(1)}, f32[8,1,256]{2,0,1:T(8,128)S(1)}, u32[]{:S(2)}, u32[]{:S(2)}) collective-permute-start(f32[8,1,256]{2,0,1:T(8,128)S(1)} %get-tuple-element.58), channel_id=1, source_target_pairs={{0,8},{8,16},{16,24},{24,32},{32,40},{40,48},{48,56},{56,64},{64,7... | collective-permute-start | bytes 24584 | tf_op jit(solution)/shard_map/ppermute | solution.py:14
  93.1 9.7 %collective-permute-start.18 = (f32[8,66,1]{2,0,1:T(8,128)S(1)}, f32[8,66,1]{2,0,1:T(8,128)S(1)}, u32[]{:S(2)}, u32[]{:S(2)}) collective-permute-start(f32[8,66,1]{2,0,1:T(8,128)S(1)} %get-tuple-element.48), channel_id=1, source_target_pairs={{0,1},{1,2},{2,3},{3,4},{4,5},{5,6},{6,7},{8,9},{9,10},{10,11},{11... | collective-permute-start | bytes 6344 | tf_op jit(solution)/shard_map/ppermute | solution.py:14
  98.0 8.9 %collective-permute-start.19 = (f32[8,66,1]{2,0,1:T(8,128)S(1)}, f32[8,66,1]{2,0,1:T(8,128)S(1)}, u32[]{:S(2)}, u32[]{:S(2)}) collective-permute-start(f32[8,66,1]{2,0,1:T(8,128)S(1)} %get-tuple-element.49), channel_id=1, source_target_pairs={{1,0},{2,1},{3,2},{4,3},{5,4},{6,5},{7,6},{9,8},{10,9},{11,10},{12... | collective-permute-start | bytes 6344 | tf_op jit(solution)/shard_map/ppermute | solution.py:17
  205.7 7.5 %collective-permute-start.22 = (f32[8,68,2]{2,0,1:T(8,128)}, f32[8,68,2]{2,0,1:T(8,128)}, u32[]{:S(2)}, u32[]{:S(2)}) collective-permute-start(f32[8,68,2]{2,0,1:T(8,128)} %get-tuple-element.40), channel_id=1, source_target_pairs={{0,1},{1,2},{2,3},{3,4},{4,5},{5,6},{6,7},{8,9},{9,10},{10,11},{11... | collective-permute-start | bytes 13064 | tf_op jit(solution)/shard_map/ppermute | solution.py:14
  208.7 9.1 %collective-permute-start.23 = (f32[8,68,2]{2,0,1:T(8,128)S(1)}, f32[8,68,2]{2,0,1:T(8,128)}, u32[]{:S(2)}, u32[]{:S(2)}) collective-permute-start(f32[8,68,2]{2,0,1:T(8,128)S(1)} %get-tuple-element.41), channel_id=1, source_target_pairs={{1,0},{2,1},{3,2},{4,3},{5,4},{6,5},{7,6},{9,8},{10,9},{11,10},{12... | collective-permute-start | bytes 13064 | tf_op jit(solution)/shard_map/ppermute | solution.py:17
  311.6 6.5 %collective-permute-start.26 = (f32[8,66,1]{2,0,1:T(8,128)S(1)}, f32[8,66,1]{2,0,1:T(8,128)S(1)}, u32[]{:S(2)}, u32[]{:S(2)}) collective-permute-start(f32[8,66,1]{2,0,1:T(8,128)S(1)} %get-tuple-element.46), channel_id=1, source_target_pairs={{0,1},{1,2},{2,3},{3,4},{4,5},{5,6},{6,7},{8,9},{9,10},{10,11},{11... | collective-permute-start | bytes 6344 | tf_op jit(solution)/shard_map/ppermute | solution.py:14
  313.2 9.1 %collective-permute-start.27 = (f32[8,66,1]{2,0,1:T(8,128)S(1)}, f32[8,66,1]{2,0,1:T(8,128)S(1)}, u32[]{:S(2)}, u32[]{:S(2)}) collective-permute-start(f32[8,66,1]{2,0,1:T(8,128)S(1)} %get-tuple-element.47), channel_id=1, source_target_pairs={{1,0},{2,1},{3,2},{4,3},{5,4},{6,5},{7,6},{9,8},{10,9},{11,10},{12... | collective-permute-start | bytes 6344 | tf_op jit(solution)/shard_map/ppermute | solution.py:17
  331.2 7.3 %collective-permute-start.30 = (f32[8,66,1]{2,0,1:T(8,128)S(1)}, f32[8,66,1]{2,0,1:T(8,128)S(1)}, u32[]{:S(2)}, u32[]{:S(2)}) collective-permute-start(f32[8,66,1]{2,0,1:T(8,128)S(1)} %get-tuple-element.44), channel_id=1, source_target_pairs={{0,1},{1,2},{2,3},{3,4},{4,5},{5,6},{6,7},{8,9},{9,10},{10,11},{11... | collective-permute-start | bytes 6344 | tf_op jit(solution)/shard_map/ppermute | solution.py:14
  333.7 9.6 %collective-permute-start.31 = (f32[8,66,1]{2,0,1:T(8,128)S(1)}, f32[8,66,1]{2,0,1:T(8,128)S(1)}, u32[]{:S(2)}, u32[]{:S(2)}) collective-permute-start(f32[8,66,1]{2,0,1:T(8,128)S(1)} %get-tuple-element.45), channel_id=1, source_target_pairs={{1,0},{2,1},{3,2},{4,3},{5,4},{6,5},{7,6},{9,8},{10,9},{11,10},{12... | collective-permute-start | bytes 6344 | tf_op jit(solution)/shard_map/ppermute | solution.py:17
  (40 other events, 426.4 us)
where the time goes:
time: 432 us; the launch traced here: 430 us
  blocking collectives  237 us (55%)
  starting transfers between devices  84.8 us (20%)
  waiting for transfers between devices  62.8 us (15%)
  other arithmetic  26.4 us (6%)
  matrix products  10.8 us (2%)
  local copies, waits for them, and re-layouts  6.61 us (2%)
    psum x1, blocking collectives, shards(): gamma = lax.psum(gram(residual, zvec), ('row', 'col'))  82.6 us
    psum x1, blocking collectives, shards(): curv = lax.psum(gram(direction, image), ('row', 'col'))  78.2 us
    psum x1, blocking collectives, shards(): gamma_new = lax.psum(gram(residual, zvec), ('row', 'col'))  76.3 us
    ppermute x16, starting transfers between devices, padded(): lax.ppermute(lax.slice_in_dim(block, block.shape[dim] - width, None, axis...  58.7 us
    ppermute x16, waiting for transfers between devices, padded(): lax.ppermute(lax.slice_in_dim(block, 0, width, axis=dim), axis, backward)  43.6 us
    ppermute x16, starting transfers between devices, padded(): lax.ppermute(lax.slice_in_dim(block, 0, width, axis=dim), axis, backward)  26.1 us
    ppermute x16, waiting for transfers between devices, padded(): lax.ppermute(lax.slice_in_dim(block, block.shape[dim] - width, None, axis...  19.2 us
  transfers between devices with their start and end apart: 32, of which 19 were waited for; matrix products, arithmetic and copies ran while one was open for 4% of the time, Pallas kernels for 0%

commit v1 on v0

v1 whole, which is shorter than its diff:
```python
import functools

import jax
import jax.numpy as jnp
from jax import lax
from jax.experimental import pallas as pl
from jax.experimental.pallas import tpu as pltpu
from jax.sharding import PartitionSpec as P

MESH = pl.DeviceIdType.MESH
PROBES = 8
LANES = 128
HALO = 8
OFF = 16
OFFSETS = [(o // 5 - 2, o % 5 - 2) for o in range(25)]


def tile_shift(tiles, place, step, lane):
    if step == 0:
        return tiles[place]
    count = len(tiles)
    here = pltpu.roll(tiles[place], (-step) % LANES, axis=1)
    if step > 0:
        there = pltpu.roll(tiles[(place + 1) % count], (-step) % LANES, axis=1)
        return jnp.where(lane < LANES - step, here, there)
    there = pltpu.roll(tiles[(place - 1) % count], (-step) % LANES, axis=1)
    return jnp.where(lane >= -step, here, there)


def ring_shifts(tiles, step, lane):
    if step == 0:
        return list(tiles)
    count = len(tiles)
    rolled = [pltpu.roll(tile, (-step) % LANES, axis=1) for tile in tiles]
    if step > 0:
        return [jnp.where(lane < LANES - step, rolled[u], rolled[(u + 1) % count]) for u in range(count)]
    return [jnp.where(lane >= -step, rolled[u], rolled[(u - 1) % count]) for u in range(count)]


def splats(matrix, first):
    out = [[None] * 8 for _ in range(8)]
    for col in range(8):
        wide = jnp.broadcast_to(matrix[:, first + col : first + col + 1], (8, LANES))
        for row in range(8):
            out[row][col] = jnp.broadcast_to(wide[row : row + 1, :], (8, LANES))
    return out


def rows_of(matrix):
    return [jnp.broadcast_to(matrix[k : k + 1, :], (8, LANES)) for k in range(8)]


def stack_rows(rows, sub):
    out = rows[0]
    for k in range(1, 8):
        out = jnp.where(sub == k, rows[k], out)
    return out


def product(left, rows):
    out = []
    for i in range(8):
        total = left[i][0] * rows[0]
        for j in range(1, 8):
            total = total + left[i][j] * rows[j]
        out.append(total)
    return out


def product_t(left, rows):
    return product([[left[j][i] for j in range(8)] for i in range(8)], rows)


def factor(entries):
    a = [list(r) for r in entries]
    mult = [[None] * 8 for _ in range(8)]
    inverse = []
    for j in range(8):
        inv = 1.0 / a[j][j]
        inverse.append(inv)
        for k in range(j + 1, 8):
            mult[k][j] = a[j][k] * inv
            for m in range(k, 8):
                a[k][m] = a[k][m] - mult[k][j] * a[j][m]
    return mult, inverse


def substitute(fact, rows):
    mult, inverse = fact
    y = list(rows)
    for j in range(8):
        for k in range(j + 1, 8):
            y[k] = y[k] - mult[k][j] * y[j]
    y = [y[j] * inverse[j] for j in range(8)]
    for j in range(7, -1, -1):
        for k in range(j):
            y[k] = y[k] - mult[j][k] * y[j]
    return y


def kernel(
    nrow, ncol, rows_n, cols_n,
    probes, kappa, conduct, inv_mass, spai, sea,
    x_out, r_out,
    rbuf, zbuf, wbuf, ybuf, tbuf, sraw, sfull, symp, cbuf, lap,
    pland, cland, seal, seaown, cpack, spack, crecv, srecv,
    grams1, grams2, coef, xs, rs,
    lsem, ssem, rsem, s1, r1, s2, r2, osem,
):
    nu = ncol // LANES
    nt = nu + 1
    row = lax.axis_index("row")
    col = lax.axis_index("col")
    core = row % 2
    pair = row // 2
    group1 = 2 * cols_n
    group2 = rows_n // 2
    up, down = (row + rows_n - 1) % rows_n, (row + 1) % rows_n
    left, right = (col + cols_n - 1) % cols_n, (col + 1) % cols_n
    mine1 = core * cols_n + col

    partners1 = []
    for d in range(1, group1):
        q = (mine1 + d) % group1
        partners1.append((row - core + q // cols_n, q % cols_n))
    partners2 = []
    for d in range(1, group2):
        q = (pair + d) % group2
        partners2.append((2 * q + core, col))
    around = [(up, left), (up, col), (up, right), (row, left), (row, right), (down, left), (down, col), (down, right)]

    barrier = pltpu.get_barrier_semaphore()
    for who in around + partners1 + partners2:
        pl.semaphore_signal(barrier, inc=1, device_id=who, device_id_type=MESH)

    local = []
    local.append(pltpu.make_async_copy(spai, sraw.at[:, pl.ds(OFF, nrow), :], lsem.at[0]))
    for u in range(nu):
        local.append(pltpu.make_async_copy(
            probes.at[:, :, pl.ds(u * LANES, LANES)], rbuf.at[u, :, pl.ds(OFF, nrow), :], lsem.at[1 + u]))
    for k, field in enumerate((kappa, conduct, inv_mass)):
        for u in range(nu):
            local.append(pltpu.make_async_copy(
                field.at[:, pl.ds(u * LANES, LANES)], cbuf.at[k, u, pl.ds(OFF, nrow), :], lsem.at[1 + nu + k * nu + u]))
    local.append(pltpu.make_async_copy(sea, seaown, lsem.at[1 + 4 * nu]))
    for copy in local:
        copy.start()

    pl.semaphore_wait(barrier, len(around) + len(partners1) + len(partners2))

    def remote(index, src, dst, who):
        return pltpu.make_async_remote_copy(
            src_ref=src, dst_ref=dst, send_sem=ssem.at[index], recv_sem=rsem.at[index],
            device_id=who, device_id_type=MESH)

    row_copies = []
    for side, who in ((0, down), (1, up)):
        first = nrow - HALO if side == 0 else 0
        first16 = nrow - OFF if side == 0 else 0
        land16 = 0 if side == 0 else OFF + nrow
        base = 6 * side
        row_copies.append(remote(base, spai.at[:, pl.ds(first16, OFF), :], sraw.at[:, pl.ds(land16, OFF), :], (who, col)))
        row_copies.append(remote(base + 1, probes.at[:, pl.ds(first, HALO), :], pland.at[side], (who, col)))
        for k, field in enumerate((kappa, conduct, inv_mass)):
            row_copies.append(remote(base + 2 + k, field.at[pl.ds(first, HALO), :], cland.at[side, k], (who, col)))
        row_copies.append(remote(base + 5, sea.at[pl.ds(first, HALO), :], seal.at[side], (who, col)))
    for copy in row_copies:
        copy.start()

    for copy in local:
        copy.wait()

    lane = lax.broadcasted_iota(jnp.int32, (8, LANES), 1)
    sub = lax.broadcasted_iota(jnp.int32, (8, LANES), 0)
    lane16 = lax.broadcasted_iota(jnp.int32, (16, LANES), 1)

    def sea_body(t, carry):
        for u in range(nu):
            rows = pl.ds(pl.multiple_of(8 * t, 8), 8)
            dst = pl.ds(pl.multiple_of(OFF + 8 * t, 8), 8)
            cbuf[3, u, dst, :] = seaown[rows, u * LANES : (u + 1) * LANES].astype(jnp.float32)
        return carry
    lax.fori_loop(0, nrow // 8, sea_body, 0)

    def pack_body(t, carry):
        src = pl.ds(pl.multiple_of(OFF + 8 * t, 8), 8)
        dst = pl.ds(pl.multiple_of(8 * t, 8), 8)
        group = lane // HALO
        for side, u in ((0, 0), (1, nu - 1)):
            total = jnp.zeros((8, LANES), jnp.float32)
            for k in range(12):
                item = rbuf[u, k, src, :] if k < 8 else cbuf[k - 8, u, src, :]
                shift = (HALO * k + (0 if side == 0 else HALO)) % LANES
                moved = pltpu.roll(item, shift, axis=1) if shift else item
                total = jnp.where(group == k, moved, total)
            cpack[side, dst, :] = total
        return carry
    lax.fori_loop(0, nrow // 8, pack_body, 0)

    def spack_body(t, carry):
        src = pl.ds(pl.multiple_of(OFF + 16 * t, 16), 16)
        dst = pl.ds(pl.multiple_of(16 * t, 16), 16)
        group = lane16 // HALO
        for o in range(25):
            tiles = []
            for u in range(nu):
                tile = sraw[o, src, u * LANES : (u + 1) * LANES].astype(jnp.float32)
                sfull[u, o, src, :] = tile
                tiles.append(tile)
            if o % 16 == 0:
                totals = [jnp.zeros((16, LANES), jnp.float32)] * 2
            for side, u in ((0, 0), (1, nu - 1)):
                shift = (HALO * o + (0 if side == 0 else HALO)) % LANES
                moved = pltpu.roll(tiles[u], shift, axis=1) if shift else tiles[u]
                totals[side] = jnp.where(group == o % 16, moved, totals[side])
            if o % 16 == 15 or o == 24:
                part = o // 16
                for side in range(2):
                    spack[side, dst, part * LANES : (part + 1) * LANES] = totals[side].astype(jnp.bfloat16)
        return carry
    lax.fori_loop(0, nrow // 16, spack_body, 0)

    col_copies = []
    for side, who in ((0, left), (1, right)):
        to = 1 - side
        base = 12 + 6 * side
        col_copies += [
            remote(base, spack.at[side], srecv.at[to, pl.ds(OFF, nrow), :], (row, who)),
            remote(base + 1, cpack.at[side], crecv.at[to, pl.ds(HALO, nrow), :], (row, who)),
            remote(base + 2, spack.at[side, pl.ds(0, OFF), :], srecv.at[to, pl.ds(OFF + nrow, OFF), :], (up, who)),
            remote(base + 3, cpack.at[side, pl.ds(0, HALO), :], crecv.at[to, pl.ds(HALO + nrow, HALO), :], (up, who)),
            remote(base + 4, spack.at[side, pl.ds(nrow - OFF, OFF), :], srecv.at[to, pl.ds(0, OFF), :], (down, who)),
            remote(base + 5, cpack.at[side, pl.ds(nrow - HALO, HALO), :], crecv.at[to, pl.ds(0, HALO), :], (down, who)),
        ]
    for copy in col_copies:
        copy.start()

    one = jnp.float32(1.0)
    zero = jnp.float32(0.0)
    has_up = jnp.where(row > 0, one, zero)
    has_down = jnp.where(row < rows_n - 1, one, zero)
    has_left = jnp.where(col > 0, one, zero)
    has_right = jnp.where(col < cols_n - 1, one, zero)

    for copy in row_copies:
        copy.wait()
    for side, keep, at in ((0, has_up, OFF - HALO), (1, has_down, OFF + nrow)):
        for u in range(nu):
            cols = slice(u * LANES, (u + 1) * LANES)
            for p in range(PROBES):
                rbuf[u, p, at : at + 8, :] = pland[side, p, :, cols] * keep
            for k in range(3):
                cbuf[k, u, at : at + 8, :] = cland[side, k, :, cols] * keep
            cbuf[3, u, at : at + 8, :] = seal[side, :, cols].astype(jnp.float32) * keep
        start = 0 if side == 0 else OFF + nrow

        def sland_body(o, carry, start=start, keep=keep):
            for u in range(nu):
                sfull[u, o, start : start + 16, :] = (
                    sraw[o, start : start + 16, u * LANES : (u + 1) * LANES].astype(jnp.float32) * keep)
            return carry
        lax.fori_loop(0, 25, sland_body, 0)

    for copy in col_copies:
        copy.wait()

    def inside_rows(first, sublane):
        at = first + sublane
        above = jnp.where(at < OFF, has_up, one)
        return jnp.where(at >= OFF + nrow, has_down, above)

    def unpack_body(t, carry):
        src = pl.ds(pl.multiple_of(8 * t, 8), 8)
        dst = pl.ds(pl.multiple_of(OFF - HALO + 8 * t, 8), 8)
        rowmask = inside_rows(OFF - HALO + 8 * t, sub)
        from_left = crecv[0, src, :] * (rowmask * has_left)
        from_right = crecv[1, src, :] * (rowmask * has_right)
        for k in range(12):
            low = pltpu.roll(from_left, (LANES - HALO - HALO * k) % LANES, axis=1)
            high = pltpu.roll(from_right, (-HALO * k) % LANES, axis=1) if k else from_right
            tile = jnp.where(lane < HALO, high, jnp.where(lane >= LANES - HALO, low, 0.0))
            if k < 8:
                rbuf[nu, k, dst, :] = tile
            else:
                cbuf[k - 8, nu, dst, :] = tile
        return carry
    lax.fori_loop(0, (nrow + 2 * HALO) // 8, unpack_body, 0)

    def sunpack_body(t, carry):
        src = pl.ds(pl.multiple_of(16 * t, 16), 16)
        rowmask = inside_rows(16 * t, lax.broadcasted_iota(jnp.int32, (16, LANES), 0))
        for part in range(2):
            cols = slice(part * LANES, (part + 1) * LANES)
            from_left = srecv[0, src, cols].astype(jnp.float32) * (rowmask * has_left)
            from_right = srecv[1, src, cols].astype(jnp.float32) * (rowmask * has_right)
            for k in range(16 if part == 0 else 9):
                low = pltpu.roll(from_left, (LANES - HALO - HALO * k) % LANES, axis=1)
                high = pltpu.roll(from_right, (-HALO * k) % LANES, axis=1) if k else from_right
                sfull[nu, 16 * part + k, src, :] = jnp.where(
                    lane16 < HALO, high, jnp.where(lane16 >= LANES - HALO, low, 0.0))
        return carry
    lax.fori_loop(0, (nrow + 2 * OFF) // 16, sunpack_body, 0)

    colmask = [jnp.ones((8, LANES), jnp.float32)] * nu + [
        jnp.where(lane < LANES // 2, has_right, has_left)]

    def sym_body(t, carry):
        at = OFF - HALO + 8 * t
        here = pl.ds(pl.multiple_of(at, 8), 8)
        rowmask = inside_rows(at, sub) * 0.5
        masks = {b: ring_shifts([m * rowmask for m in colmask], -b, lane) for b in range(-2, 3)}
        for o, (a, b) in enumerate(OFFSETS):
            own = ring_shifts([sfull[u, o, here, :] for u in range(nt)], -b, lane)
            for u in range(nt):
                mirror = sfull[u, 24 - o, pl.ds(at + a, 8), :]
                symp[u, o, here, :] = (own[u] + mirror) * masks[b][u]
        return carry
    lax.fori_loop(0, (nrow + 2 * HALO) // 8, sym_body, 0)

    def lap_body(t, carry):
        at = OFF - HALO + 8 * t
        here = pl.ds(pl.multiple_of(at, 8), 8)
        above, below = pl.ds(at - 1, 8), pl.ds(at + 1, 8)
        tiles = lambda k, rows: [cbuf[k, u, rows, :] for u in range(nt)]
        kap, con, inv, msk = (tiles(k, here) for k in range(4))
        con_n = ring_shifts(con, 1, lane)
        east = [0.5 * (con[u] + con_n[u]) for u in range(nt)]
        west = ring_shifts(east, -1, lane)
        inv_e, inv_w = ring_shifts(inv, 1, lane), ring_shifts(inv, -1, lane)
        msk_e, msk_w = ring_shifts(msk, 1, lane), ring_shifts(msk, -1, lane)
        for u in range(nt):
            north = 0.5 * (con[u] + cbuf[1, u, above, :])
            south = 0.5 * (con[u] + cbuf[1, u, below, :])
            diag = kap[u] + north + south + west[u] + east[u]
            lap[0, u, here, :] = inv[u] * diag * msk[u]
            lap[1, u, here, :] = inv[u] * north * cbuf[3, u, above, :]
            lap[2, u, here, :] = inv[u] * south * cbuf[3, u, below, :]
            lap[3, u, here, :] = inv_w[u] * west[u] * msk[u]
            lap[4, u, here, :] = inv_e[u] * east[u] * msk[u]
            lap[5, u, here, :] = msk[u] * diag
            lap[6, u, here, :] = msk[u] * north
            lap[7, u, here, :] = msk[u] * south
            lap[8, u, here, :] = msk_w[u] * west[u]
            lap[9, u, here, :] = msk_e[u] * east[u]
            lap[10, u, here, :] = 1.0 - msk[u]
        return carry
    lax.fori_loop(0, (nrow + 2 * HALO) // 8, lap_body, 0)

    def apply_m(src, dst, start, count):
        def body(t, carry):
            at = start + 8 * t
            for p0 in range(0, PROBES, 2):
                pair_p = (p0, p0 + 1)
                field = {(p, a, u): src[u, p, pl.ds(at + a, 8), :] for p in pair_p for a in range(-2, 3) for u in range(nt)}
                total = {}
                for b in range(-2, 3):
                    part = {}
                    for a in range(-2, 3):
                        o = (a + 2) * 5 + b + 2
                        for u in range(nt):
                            weight = symp[u, o, pl.ds(at, 8), :]
                            for p in pair_p:
                                term = weight * field[p, a, u]
                                part[p, u] = term if a == -2 else part[p, u] + term
                    for p in pair_p:
                        moved = ring_shifts([part[p, u] for u in range(nt)], b, lane)
                        for u in range(nt):
                            total[p, u] = moved[u] if b == -2 else total[p, u] + moved[u]
                for p in pair_p:
                    for u in range(nt):
                        dst[u, p, pl.ds(at, 8), :] = total[p, u]
            return carry
        lax.fori_loop(0, count, body, 0)

    def half_laplace(first, src, at, p, coefs):
        centre = [src[u, p, pl.ds(at, 8), :] for u in range(nt)]
        to_east = ring_shifts([coefs[3][u] * centre[u] for u in range(nt)], 1, lane)
        to_west = ring_shifts([coefs[4][u] * centre[u] for u in range(nt)], -1, lane)
        out = []
        for u in range(nt):
            across = to_east[u] + to_west[u]
            along = coefs[1][u] * src[u, p, pl.ds(at - 1, 8), :] + coefs[2][u] * src[u, p, pl.ds(at + 1, 8), :]
            out.append(coefs[0][u] * centre[u] - (across + along))
        return out

    def apply_a(src, dst, start_in, count_in, start, count, keep):
        def inner(t, carry):
            at = start_in + 8 * t
            coefs = [[lap[k, u, pl.ds(at, 8), :] for u in range(nt)] for k in range(5)]
            for p in range(PROBES):
                out = half_laplace(0, src, at, p, coefs)
                for u in range(nt):
                    tbuf[u, p, pl.ds(at, 8), :] = out[u]
            return carry
        lax.fori_loop(0, count_in, inner, 0)

        def outer(t, carry):
            at = start + 8 * t
            coefs = [[lap[5 + k, u, pl.ds(at, 8), :] for u in range(nt)] for k in range(6)]
            for p in range(PROBES):
                out = half_laplace(5, tbuf, at, p, coefs)
                for u in range(keep):
                    dst[u, p, pl.ds(at, 8), :] = out[u] + coefs[5][u] * src[u, p, pl.ds(at, 8), :]
            return carry
        lax.fori_loop(0, count, outer, 0)

    pairs = [(k, l) for k in range(8) for l in range(k, 8)]

    def gram(first, second):
        def body(i, acc):
            u = i // (nrow // 8)
            rows = pl.ds(pl.multiple_of(OFF + 8 * (i % (nrow // 8)), 8), 8)
            a = [first[u, p, rows, :] for p in range(PROBES)]
            b = [second[u, p, rows, :] for p in range(PROBES)]
            return tuple(acc[n] + a[k] * b[l] for n, (k, l) in enumerate(pairs))
        start = tuple(jnp.zeros((8, LANES), jnp.float32) for _ in pairs)
        acc = lax.fori_loop(0, nu * (nrow // 8), body, start)
        return [jnp.sum(a, axis=0, keepdims=True) for a in acc]

    def gather(total, m, sums):
        index = {}
        for n, (k, l) in enumerate(pairs):
            index[k, l] = index[l, k] = sums[n]
        for l in range(8):
            stacked = jnp.broadcast_to(index[0, l], (8, LANES))
            for k in range(1, 8):
                stacked = jnp.where(sub == k, index[k, l], stacked)
            total = jnp.where(lane == 8 * m + l, jnp.sum(stacked, axis=1, keepdims=True), total)
        return total

    last = nrow + OFF
    partial = jnp.zeros((8, LANES), jnp.float32)
    apply_m(rbuf, zbuf, OFF - 8, (nrow + 16) // 8)
    partial = gather(partial, 0, gram(rbuf, zbuf))
    apply_a(zbuf, wbuf, OFF - 8, (nrow + 16) // 8, OFF - 4, (nrow + 8) // 8, nt)
    partial = gather(partial, 1, gram(zbuf, wbuf))
    apply_m(wbuf, ybuf, OFF - 2, (nrow + 8) // 8)
    partial = gather(partial, 2, gram(wbuf, ybuf))
    vbuf = sfull
    apply_a(ybuf, vbuf, OFF - 1, (nrow + 8) // 8, OFF, nrow // 8, nu)
    partial = gather(partial, 3, gram(ybuf, vbuf))

    def exchange(value, buf, mine, partners, ssems, rsems, count):
        buf[mine] = value
        copies = []
        for d, who in enumerate(partners):
            copies.append(pltpu.make_async_remote_copy(
                src_ref=buf.at[mine], dst_ref=buf.at[mine], send_sem=ssems.at[d], recv_sem=rsems.at[mine],
                device_id=who, device_id_type=MESH))
        for copy in copies:
            copy.start()
        for d in range(1, count):
            slot = (mine + d) % count
            pltpu.make_async_copy(buf.at[slot], buf.at[slot], rsems.at[slot]).wait()
        for copy in copies:
            copy.wait_send()
        total = buf[0]
        for k in range(1, count):
            total = total + buf[k]
        return total

    g = exchange(partial, grams1, mine1, partners1, s1, r1, group1)
    g = exchange(g, grams2, pair, partners2, s2, r2, group2)

    g1s, g2s, g3s, g4s = (splats(g, 8 * m) for m in range(4))
    shifted = lambda m: pltpu.roll(g, (-8 * m) % LANES, axis=1) if m else g
    g1r, g2r = rows_of(shifted(0)), rows_of(shifted(1))
    fact2, fact1 = factor(g2s), factor(g1s)
    add = lambda x, y: [a + b for a, b in zip(x, y)]
    minus = lambda x, y: [a - b for a, b in zip(x, y)]
    alpha = substitute(fact2, g1r)
    alpha_s = splats(stack_rows(alpha, sub), 0)
    g3_alpha = product(g3s, alpha)
    gamma = minus(minus(g1r, product(g2s, alpha)), product_t(alpha_s, minus(g2r, g3_alpha)))
    beta = substitute(fact1, gamma)
    eye = [jnp.where(lane == k, 1.0, 0.0) for k in range(8)]
    b_rows = add(beta, eye)
    b_s = splats(stack_rows(b_rows, sub), 0)
    curv = minus(
        product_t(b_s, minus(product(g2s, b_rows), g3_alpha)),
        product_t(alpha_s, minus(product(g3s, b_rows), product(g4s, alpha))))
    curv_s = splats(stack_rows(curv, sub), 0)
    curv_s = [[0.5 * (curv_s[k][l] + curv_s[l][k]) for l in range(8)] for k in range(8)]
    alpha1 = substitute(factor(curv_s), gamma)
    c1 = add(alpha, product(b_s, alpha1))
    c2 = product(alpha_s, alpha1)
    for m, rows in enumerate((c1, c2)):
        spread = splats(stack_rows(rows, sub), 0)
        for k in range(8):
            for l in range(8):
                coef[m, l, k] = spread[k][l]

    outs = []
    for l in range(PROBES):
        outs.append(pltpu.make_async_copy(xs.at[l], x_out.at[l], osem.at[l]))
        outs.append(pltpu.make_async_copy(rs.at[l], r_out.at[l], osem.at[8 + l]))
    for l0 in range(0, PROBES, 2):
        ca = [[coef[0, l, k] for k in range(8)] for l in (l0, l0 + 1)]
        cb = [[coef[1, l, k] for k in range(8)] for l in (l0, l0 + 1)]

        def mix_body(t, carry, l0=l0, ca=ca, cb=cb):
            rows = pl.ds(pl.multiple_of(OFF + 8 * t, 8), 8)
            out = pl.ds(pl.multiple_of(8 * t, 8), 8)
            for u in range(nu):
                cols = slice(u * LANES, (u + 1) * LANES)
                for first, second, dst, base, sign in ((zbuf, ybuf, xs, None, 1.0), (wbuf, vbuf, rs, rbuf, -1.0)):
                    f = [first[u, k, rows, :] for k in range(8)]
                    s = [second[u, k, rows, :] for k in range(8)]
                    for i in range(2):
                        total = ca[i][0] * f[0]
                        for k in range(1, 8):
                            total = total + ca[i][k] * f[k]
                        for k in range(8):
                            total = total - cb[i][k] * s[k]
                        if base is not None:
                            total = base[u, l0 + i, rows, :] - total
                        dst[l0 + i, out, cols] = total
            return carry
        lax.fori_loop(0, nrow // 8, mix_body, 0)
        for copy in outs[2 * l0 : 2 * l0 + 4]:
            copy.start()
    for copy in outs:
        copy.wait()


def shards(probes, kappa_sq, conduct, inv_mass, spai, sea_mask):
    _, nrow, ncol = probes.shape
    rows_n, cols_n = lax.axis_size("row"), lax.axis_size("col")
    nu = ncol // LANES
    nt = nu + 1
    ext = nrow + 2 * OFF
    f32, bf16 = jnp.float32, jnp.bfloat16
    field = pltpu.VMEM((nt, PROBES, ext, LANES), f32)
    dma = pltpu.SemaphoreType.DMA
    scratch = [
        field, field, field, field, field,
        pltpu.VMEM((25, ext, ncol), bf16),
        pltpu.VMEM((nt, 25, ext, LANES), f32),
        pltpu.VMEM((nt, 25, ext, LANES), f32),
        pltpu.VMEM((4, nt, ext, LANES), f32),
        pltpu.VMEM((11, nt, ext, LANES), f32),
        pltpu.VMEM((2, PROBES, HALO, ncol), f32),
        pltpu.VMEM((2, 3, HALO, ncol), f32),
        pltpu.VMEM((2, HALO, ncol), jnp.int32),
        pltpu.VMEM((nrow, ncol), jnp.int32),
        pltpu.VMEM((2, nrow, LANES), f32),
        pltpu.VMEM((2, nrow, 2 * LANES), bf16),
        pltpu.VMEM((2, nrow + 2 * HALO, LANES), f32),
        pltpu.VMEM((2, ext, 2 * LANES), bf16),
        pltpu.VMEM((2 * cols_n, 8, LANES), f32),
        pltpu.VMEM((rows_n // 2, 8, LANES), f32),
        pltpu.VMEM((2, 8, 8, 8, LANES), f32),
        pltpu.VMEM((PROBES, nrow, ncol), f32),
        pltpu.VMEM((PROBES, nrow, ncol), f32),
        dma((2 + 4 * nu,)),
        dma((24,)), dma((24,)),
        dma((2 * cols_n,)), dma((2 * cols_n,)),
        dma((rows_n // 2,)), dma((rows_n // 2,)),
        dma((16,)),
    ]
    out = jax.ShapeDtypeStruct(probes.shape, f32)
    return pl.pallas_call(
        functools.partial(kernel, nrow, ncol, rows_n, cols_n),
        out_shape=(out, out),
        in_specs=[pl.BlockSpec(memory_space=pl.ANY)] * 6,
        out_specs=(pl.BlockSpec(memory_space=pl.ANY),) * 2,
        scratch_shapes=scratch,
        compiler_params=pltpu.CompilerParams(
            collective_id=0, has_side_effects=True, vmem_limit_bytes=48 * 1024 * 1024),
    )(probes, kappa_sq, conduct, inv_mass, spai, sea_mask)


def solution(mesh):
    field = P(None, "row", "col")
    cell = P("row", "col")
    return jax.shard_map(
        shards, mesh=mesh, in_specs=(field, cell, cell, cell, field, cell),
        out_specs=(field, field), check_vma=False)
```

time: 432 us -> 58.1 us (0.13)
  blocking collectives: 237 us -> 0 us
  starting transfers between devices: 84.8 us -> 0 us
  waiting for transfers between devices: 62.8 us -> 0 us
  Pallas kernels: 0 us -> 50 us
  other arithmetic: 26.4 us -> 0 us
  matrix products: 10.8 us -> 0 us
    psum x3 -> x0, blocking collectives: 237 us -> none  [the longest x1 82.6 us: shards(): gamma = lax.psum(gram(residual, zvec), ('row', 'col'))]
    ppermute x32 -> x0, starting transfers between devices: 84.8 us -> none  [the longest x16 58.7 us: padded(): lax.ppermute(lax.slice_in_dim(block, block.shape[dim] - width, None, axis...]
    ppermute x32 -> x0, waiting for transfers between devices: 62.8 us -> none  [the longest x16 43.6 us: padded(): lax.ppermute(lax.slice_in_dim(block, 0, width, axis=dim), axis, backward)]
    pallas_call x0 -> x1, Pallas kernels: none -> 50 us  [shards(): pl.pallas_call(functools.partial(kernel, nrow, ncol, rows_n, cols_n), out...]
    another operation x15 -> x0, other arithmetic: 9.08 us -> none  [the longest x9 4.75 us: solve_small(): factor = jnp.linalg.cholesky(matrix)]
    dot_general x9 -> x0, matrix products: 8.25 us -> none  [the longest x4 5.17 us: gram(): jnp.einsum('kij,lij->kl', left, right, precision=lax.Precision.HIGHEST)]
    mul x15 -> x0, other arithmetic: 7.54 us -> none  [the longest x1 5.24 us: shards(): masked = sea[None] * direction]
    unnamed x69 -> x14, local copies, waits for them, and re-layouts: 2.07 us -> 7.12 us
  transfers between devices with their start and end apart: 32 -> 0, of which waited for: 19 -> 0; matrix products, arithmetic and copies ran while one was open for 4% -> 0% of each run, Pallas kernels for 0% -> 0%
where the time goes in v1:
time: 58.1 us; the launch traced here: 57.8 us
  Pallas kernels  50 us (86%)
  local copies, waits for them, and re-layouts  7.12 us (12%)
  between operations  0.65 us (1%)
    pallas_call x1, Pallas kernels, shards(): pl.pallas_call(functools.partial(kernel, nrow, ncol, rows_n, cols_n), out...  50 us
    unnamed x14, local copies, waits for them, and re-layouts  7.12 us

profile of v1, /device:TPU:1, one launch (start us, length us, event | category | flops | bytes accessed | tf_op | source)
XLA Modules:
  0.0 57.8 jit_solution(1370708303405639935)
XLA Ops:
  0.6 0.0 copy-start
  0.6 1.1 %copy-done = bf16[25,64,256]{2,1,0:T(8,128)(2,1)S(1)} copy-done((bf16[25,64,256]{2,1,0:T(8,128)(2,1)S(1)}, bf16[25,64,256]{2,1,0:T(8,128)(2,1)}, u32[]{:S(2)}) %copy-start) | copy-done | bytes 819224
  1.8 0.0 copy-start.1
  1.8 1.0 %copy-done.1 = f32[8,64,256]{2,1,0:T(8,128)S(1)} copy-done((f32[8,64,256]{2,1,0:T(8,128)S(1)}, f32[8,64,256]{2,1,0:T(8,128)}, u32[]{:S(2)}) %copy-start.1) | copy-done | bytes 524312
  2.8 0.0 copy-start.2
  2.8 0.8 %copy-done.2 = f32[64,256]{1,0:T(8,128)S(1)} copy-done((f32[64,256]{1,0:T(8,128)S(1)}, f32[64,256]{1,0:T(8,128)}, u32[]{:S(2)}) %copy-start.2) | copy-done | bytes 65560
  3.7 0.0 copy-start.3
  3.7 0.8 %copy-done.3 = f32[64,256]{1,0:T(8,128)S(1)} copy-done((f32[64,256]{1,0:T(8,128)S(1)}, f32[64,256]{1,0:T(8,128)}, u32[]{:S(2)}) %copy-start.3) | copy-done | bytes 65560
  4.5 0.0 copy-start.4
  4.5 0.8 %copy-done.4 = f32[64,256]{1,0:T(8,128)S(1)} copy-done((f32[64,256]{1,0:T(8,128)S(1)}, f32[64,256]{1,0:T(8,128)}, u32[]{:S(2)}) %copy-start.4) | copy-done | bytes 65560
  5.3 0.0 copy-start.5
  5.3 0.8 %copy-done.5 = s32[64,256]{1,0:T(8,128)S(1)} copy-done((s32[64,256]{1,0:T(8,128)S(1)}, s32[64,256]{1,0:T(8,128)}, u32[]{:S(2)}) %copy-start.5) | copy-done | bytes 65560
  6.2 50.0 %shard_map.77 = (f32[8,64,256]{2,1,0:T(8,128)S(1)}, f32[8,64,256]{2,1,0:T(8,128)S(1)}) custom-call(f32[8,64,256]{2,1,0:T(8,128)S(1)} %copy-done.1, f32[64,256]{1,0:T(8,128)S(1)} %copy-done.2, f32[64,256]{1,0:T(8,128)S(1)} %copy-done.3, f32[64,256]{1,0:T(8,128)S(1)} %copy-done.4, bf16[25,64,256]{2,1,0:T(8,128)(2,1)S(1)} %copy-done, s32[64,256]{1,0:T(8,128)S(1)} %copy-done.5), custom_call_target="tpu_custom_call" | custom-call | tf_op jit(solution)/shard_map/pallas_call | solution.py:562
  56.2 0.8 %copy.10 = f32[8,64,256]{2,1,0:T(8,128)} copy(f32[8,64,256]{2,1,0:T(8,128)S(1)} %get-tuple-element.4) | data formatting | bytes 1048576
  57.0 0.8 %copy.11 = f32[8,64,256]{2,1,0:T(8,128)} copy(f32[8,64,256]{2,1,0:T(8,128)S(1)} %get-tuple-element.5) | data formatting | bytes 1048576
Async XLA Ops:
  0.6 1.1 %copy-start = (bf16[25,64,256]{2,1,0:T(8,128)(2,1)S(1)}, bf16[25,64,256]{2,1,0:T(8,128)(2,1)}, u32[]{:S(2)}) copy-start(bf16[25,64,256]{2,1,0:T(8,128)(2,1)} %spai.1) | copy-start | bytes 2457604
  1.8 1.0 %copy-start.1 = (f32[8,64,256]{2,1,0:T(8,128)S(1)}, f32[8,64,256]{2,1,0:T(8,128)}, u32[]{:S(2)}) copy-start(f32[8,64,256]{2,1,0:T(8,128)} %probes.1) | copy-start | bytes 1572868
  2.8 0.8 %copy-start.2 = (f32[64,256]{1,0:T(8,128)S(1)}, f32[64,256]{1,0:T(8,128)}, u32[]{:S(2)}) copy-start(f32[64,256]{1,0:T(8,128)} %kappa.1) | copy-start | bytes 196612
  3.7 0.8 %copy-start.3 = (f32[64,256]{1,0:T(8,128)S(1)}, f32[64,256]{1,0:T(8,128)}, u32[]{:S(2)}) copy-start(f32[64,256]{1,0:T(8,128)} %conduct.1) | copy-start | bytes 196612
  4.5 0.8 %copy-start.4 = (f32[64,256]{1,0:T(8,128)S(1)}, f32[64,256]{1,0:T(8,128)}, u32[]{:S(2)}) copy-start(f32[64,256]{1,0:T(8,128)} %inv_mass.1) | copy-start | bytes 196612
  5.3 0.8 %copy-start.5 = (s32[64,256]{1,0:T(8,128)S(1)}, s32[64,256]{1,0:T(8,128)}, u32[]{:S(2)}) copy-start(s32[64,256]{1,0:T(8,128)} %sea.1) | copy-start | bytes 196612

commit v2 on v1

v2 whole, which is shorter than its diff:
```python
import functools

import jax
import jax.numpy as jnp
from jax import lax
from jax.experimental import pallas as pl
from jax.experimental.pallas import tpu as pltpu
from jax.sharding import PartitionSpec as P

MESH = pl.DeviceIdType.MESH
PROBES = 8
LANES = 128
HALO = 8
OFF = 16
OFFSETS = [(o // 5 - 2, o % 5 - 2) for o in range(25)]


def tile_shift(tiles, place, step, lane):
    if step == 0:
        return tiles[place]
    count = len(tiles)
    here = pltpu.roll(tiles[place], (-step) % LANES, axis=1)
    if step > 0:
        there = pltpu.roll(tiles[(place + 1) % count], (-step) % LANES, axis=1)
        return jnp.where(lane < LANES - step, here, there)
    there = pltpu.roll(tiles[(place - 1) % count], (-step) % LANES, axis=1)
    return jnp.where(lane >= -step, here, there)


def ring_shifts(tiles, step, lane):
    if step == 0:
        return list(tiles)
    count = len(tiles)
    rolled = [pltpu.roll(tile, (-step) % LANES, axis=1) for tile in tiles]
    if step > 0:
        return [jnp.where(lane < LANES - step, rolled[u], rolled[(u + 1) % count]) for u in range(count)]
    return [jnp.where(lane >= -step, rolled[u], rolled[(u - 1) % count]) for u in range(count)]


def splats(matrix, first):
    out = [[None] * 8 for _ in range(8)]
    for col in range(8):
        wide = jnp.broadcast_to(matrix[:, first + col : first + col + 1], (8, LANES))
        for row in range(8):
            out[row][col] = jnp.broadcast_to(wide[row : row + 1, :], (8, LANES))
    return out


def rows_of(matrix):
    return [jnp.broadcast_to(matrix[k : k + 1, :], (8, LANES)) for k in range(8)]


def stack_rows(rows, sub):
    out = rows[0]
    for k in range(1, 8):
        out = jnp.where(sub == k, rows[k], out)
    return out


def product(left, rows):
    out = []
    for i in range(8):
        total = left[i][0] * rows[0]
        for j in range(1, 8):
            total = total + left[i][j] * rows[j]
        out.append(total)
    return out


def product_t(left, rows):
    return product([[left[j][i] for j in range(8)] for i in range(8)], rows)


def factor(entries):
    a = [list(r) for r in entries]
    mult = [[None] * 8 for _ in range(8)]
    inverse = []
    for j in range(8):
        inv = 1.0 / a[j][j]
        inverse.append(inv)
        for k in range(j + 1, 8):
            mult[k][j] = a[j][k] * inv
            for m in range(k, 8):
                a[k][m] = a[k][m] - mult[k][j] * a[j][m]
    return mult, inverse


def substitute(fact, rows):
    mult, inverse = fact
    y = list(rows)
    for j in range(8):
        for k in range(j + 1, 8):
            y[k] = y[k] - mult[k][j] * y[j]
    y = [y[j] * inverse[j] for j in range(8)]
    for j in range(7, -1, -1):
        for k in range(j):
            y[k] = y[k] - mult[j][k] * y[j]
    return y


def kernel(
    nrow, ncol, rows_n, cols_n,
    probes, kappa, conduct, inv_mass, spai, sea,
    x_out, r_out,
    rbuf, zbuf, wbuf, ybuf, tbuf, sraw, sfull, symp, cbuf, lap,
    fedge, sedge, fland, sland, seaown, cpack, spack, crecv, srecv,
    grams, coef, xs, rs, ps, ws, vbuf,
    lsem, ssem, rsem, gsend, grecv, osem,
):
    nu = ncol // LANES
    nt = nu + 1
    row = lax.axis_index("row")
    col = lax.axis_index("col")
    core = row % 2
    pair = row // 2
    group1 = 2 * cols_n
    group2 = rows_n // 2
    up, down = (row + rows_n - 1) % rows_n, (row + 1) % rows_n
    left, right = (col + cols_n - 1) % cols_n, (col + 1) % cols_n
    mine1 = core * cols_n + col

    partners1 = []
    for d in range(1, group1):
        q = (mine1 + d) % group1
        partners1.append((row - core + q // cols_n, q % cols_n))
    partners2 = []
    for d in range(1, group2):
        q = (pair + d) % group2
        partners2.append((2 * q + core, col))
    around = [(up, left), (up, col), (up, right), (row, left), (row, right), (down, left), (down, col), (down, right)]

    barrier = pltpu.get_barrier_semaphore()
    for who in around + partners1 + partners2:
        pl.semaphore_signal(barrier, inc=1, device_id=who, device_id_type=MESH)

    local = []
    local.append(pltpu.make_async_copy(spai, sraw, lsem.at[0]))
    for u in range(nu):
        local.append(pltpu.make_async_copy(
            probes.at[:, :, pl.ds(u * LANES, LANES)], rbuf.at[u, :, pl.ds(OFF, nrow), :], lsem.at[1 + u]))
    for k, field in enumerate((kappa, conduct, inv_mass)):
        for u in range(nu):
            local.append(pltpu.make_async_copy(
                field.at[:, pl.ds(u * LANES, LANES)], cbuf.at[k, u, pl.ds(OFF, nrow), :], lsem.at[1 + nu + k * nu + u]))
    local.append(pltpu.make_async_copy(sea, seaown, lsem.at[1 + 4 * nu]))
    for copy in local:
        copy.start()

    lane = lax.broadcasted_iota(jnp.int32, (8, LANES), 1)
    sub = lax.broadcasted_iota(jnp.int32, (8, LANES), 0)
    lane16 = lax.broadcasted_iota(jnp.int32, (16, LANES), 1)
    edge_lanes = jnp.logical_or(lane < HALO, lane >= LANES - HALO)
    edge_lanes16 = jnp.logical_or(lane16 < HALO, lane16 >= LANES - HALO)

    for copy in local[1:]:
        copy.wait()

    def sea_body(t, carry):
        for u in range(nu):
            rows = pl.ds(pl.multiple_of(8 * t, 8), 8)
            dst = pl.ds(pl.multiple_of(OFF + 8 * t, 8), 8)
            cbuf[3, u, dst, :] = seaown[rows, u * LANES : (u + 1) * LANES].astype(jnp.float32)
        return carry
    lax.fori_loop(0, nrow // 8, sea_body, 0)

    for side, at in ((0, OFF + nrow - HALO), (1, OFF)):
        for u in range(nu):
            cols = slice(u * LANES, (u + 1) * LANES)
            for k in range(12):
                fedge[side, k, :, cols] = rbuf[u, k, at : at + 8, :] if k < 8 else cbuf[k - 8, u, at : at + 8, :]

    def pack_body(t, carry):
        src = pl.ds(pl.multiple_of(OFF + 8 * t, 8), 8)
        dst = pl.ds(pl.multiple_of(8 * t, 8), 8)
        group = lane // HALO
        for side, u in ((0, 0), (1, nu - 1)):
            total = jnp.zeros((8, LANES), jnp.float32)
            for k in range(12):
                item = rbuf[u, k, src, :] if k < 8 else cbuf[k - 8, u, src, :]
                moved = pltpu.roll(item, HALO * k, axis=1) if k else item
                total = jnp.where(group == (k - side) % 16, moved, total)
            cpack[side, dst, :] = total
        return carry
    lax.fori_loop(0, nrow // 8, pack_body, 0)

    local[0].wait()

    def spack_body(t, carry):
        src = pl.ds(pl.multiple_of(16 * t, 16), 16)
        full = pl.ds(pl.multiple_of(OFF + 16 * t, 16), 16)
        group = lane16 // HALO
        for o in range(25):
            tiles = []
            for u in range(nu):
                tile = sraw[o, src, u * LANES : (u + 1) * LANES].astype(jnp.float32)
                sfull[u, o, full, :] = tile
                tiles.append(tile)
            if o % 16 == 0:
                totals = [jnp.zeros((16, LANES), jnp.float32)] * 2
            for side, u in ((0, 0), (1, nu - 1)):
                shift = (HALO * o) % LANES
                moved = pltpu.roll(tiles[u], shift, axis=1) if shift else tiles[u]
                totals[side] = jnp.where(group == (o - side) % 16, moved, totals[side])
            if o % 16 == 15 or o == 24:
                part = o // 16
                for side in range(2):
                    spack[side, src, part * LANES : (part + 1) * LANES] = totals[side].astype(jnp.bfloat16)
        return carry
    lax.fori_loop(0, nrow // 16, spack_body, 0)

    for side, at in ((0, OFF + nrow - HALO), (1, OFF)):
        for u in range(nu):
            cols = slice(u * LANES, (u + 1) * LANES)
            for j in range(13):
                first = sfull[u, 2 * j, at : at + 8, :]
                second = sfull[u, min(2 * j + 1, 24), at : at + 8, :]
                sedge[side, j, :, cols] = jnp.concatenate([first, second], axis=0).astype(jnp.bfloat16)

    pl.semaphore_wait(barrier, len(around) + len(partners1) + len(partners2))

    def remote(index, src, dst, who):
        return pltpu.make_async_remote_copy(
            src_ref=src, dst_ref=dst, send_sem=ssem.at[index], recv_sem=rsem.at[index],
            device_id=who, device_id_type=MESH)

    row_copies = []
    for side, who in ((0, down), (1, up)):
        row_copies.append(remote(2 * side, sedge.at[side], sland.at[side], (who, col)))
        row_copies.append(remote(2 * side + 1, fedge.at[side], fland.at[side], (who, col)))
    col_copies = []
    for side, who in ((0, left), (1, right)):
        to = 1 - side
        base = 4 + 6 * side
        col_copies += [
            remote(base, spack.at[side, pl.ds(0, OFF), :], srecv.at[to, pl.ds(OFF + nrow, OFF), :], (up, who)),
            remote(base + 1, cpack.at[side, pl.ds(0, HALO), :], crecv.at[to, pl.ds(HALO + nrow, HALO), :], (up, who)),
            remote(base + 2, spack.at[side, pl.ds(nrow - OFF, OFF), :], srecv.at[to, pl.ds(0, OFF), :], (down, who)),
            remote(base + 3, cpack.at[side, pl.ds(nrow - HALO, HALO), :], crecv.at[to, pl.ds(0, HALO), :], (down, who)),
            remote(base + 4, spack.at[side], srecv.at[to, pl.ds(OFF, nrow), :], (row, who)),
            remote(base + 5, cpack.at[side], crecv.at[to, pl.ds(HALO, nrow), :], (row, who)),
        ]
    for copy in col_copies + row_copies:
        copy.start()

    one = jnp.float32(1.0)
    zero = jnp.float32(0.0)
    has_up = jnp.where(row > 0, one, zero)
    has_down = jnp.where(row < rows_n - 1, one, zero)
    has_left = jnp.where(col > 0, one, zero)
    has_right = jnp.where(col < cols_n - 1, one, zero)

    def rotate_body(t, carry):
        here = pl.ds(pl.multiple_of(OFF + 8 * t, 8), 8)
        for o, (a, b) in enumerate(OFFSETS):
            if b:
                for u in range(nu):
                    symp[u, o, here, :] = pltpu.roll(sfull[u, o, here, :], b % LANES, axis=1)
        return carry
    lax.fori_loop(0, nrow // 8, rotate_body, 0)

    for copy in row_copies:
        copy.wait_recv()
    for side, keep, at in ((0, has_up, OFF - HALO), (1, has_down, OFF + nrow)):
        for u in range(nu):
            cols = slice(u * LANES, (u + 1) * LANES)
            for k in range(12):
                item = fland[side, k, :, cols] * keep
                if k < 8:
                    rbuf[u, k, at : at + 8, :] = item
                else:
                    cbuf[k - 8, u, at : at + 8, :] = item
            for j in range(13):
                both = sland[side, j, :, cols].astype(jnp.float32) * keep
                sfull[u, 2 * j, at : at + 8, :] = both[0:8]
                if j < 12:
                    sfull[u, 2 * j + 1, at : at + 8, :] = both[8:16]

    for copy in col_copies:
        copy.wait_recv()

    def inside_rows(first, sublane):
        at = first + sublane
        above = jnp.where(at < OFF, has_up, one)
        return jnp.where(at >= OFF + nrow, has_down, above)

    def unpack_body(t, carry):
        src = pl.ds(pl.multiple_of(8 * t, 8), 8)
        dst = pl.ds(pl.multiple_of(OFF - HALO + 8 * t, 8), 8)
        rowmask = inside_rows(OFF - HALO + 8 * t, sub)
        from_left = crecv[0, src, :] * (rowmask * has_left)
        from_right = crecv[1, src, :] * (rowmask * has_right)
        odd = (lane // HALO) % 2 == 1
        merged = (jnp.where(odd, from_left, from_right), jnp.where(odd, from_right, from_left))
        for k in range(12):
            moved = pltpu.roll(merged[k % 2], (-HALO * k) % LANES, axis=1) if k else merged[0]
            tile = jnp.where(edge_lanes, moved, 0.0)
            if k < 8:
                rbuf[nu, k, dst, :] = tile
            else:
                cbuf[k - 8, nu, dst, :] = tile
        return carry
    lax.fori_loop(0, (nrow + 2 * HALO) // 8, unpack_body, 0)

    def sunpack_body(t, carry):
        src = pl.ds(pl.multiple_of(16 * t, 16), 16)
        rowmask = inside_rows(16 * t, lax.broadcasted_iota(jnp.int32, (16, LANES), 0))
        for part in range(2):
            cols = slice(part * LANES, (part + 1) * LANES)
            from_left = srecv[0, src, cols].astype(jnp.float32) * (rowmask * has_left)
            from_right = srecv[1, src, cols].astype(jnp.float32) * (rowmask * has_right)
            odd = (lane16 // HALO) % 2 == 1
            merged = (jnp.where(odd, from_left, from_right), jnp.where(odd, from_right, from_left))
            for k in range(16 if part == 0 else 9):
                moved = pltpu.roll(merged[k % 2], (-HALO * k) % LANES, axis=1) if k else merged[0]
                sfull[nu, 16 * part + k, src, :] = jnp.where(edge_lanes16, moved, 0.0)
        return carry
    lax.fori_loop(0, (nrow + 2 * OFF) // 16, sunpack_body, 0)

    colmask = [jnp.ones((8, LANES), jnp.float32)] * nu + [
        jnp.where(lane < LANES // 2, has_right, has_left)]

    def sym_tile(at, rotated):
        here = pl.ds(at, 8)
        rowmask = inside_rows(at, sub) * 0.5
        masks = {b: ring_shifts([m * rowmask for m in colmask], -b, lane) for b in range(-2, 3)}
        for o, (a, b) in enumerate(OFFSETS):
            if b == 0:
                own = [sfull[u, o, here, :] for u in range(nt)]
            else:
                rolled = [
                    symp[u, o, here, :] if rotated and u < nu else pltpu.roll(sfull[u, o, here, :], b % LANES, axis=1)
                    for u in range(nt)]
                if b < 0:
                    own = [jnp.where(lane < LANES + b, rolled[u], rolled[(u + 1) % nt]) for u in range(nt)]
                else:
                    own = [jnp.where(lane >= b, rolled[u], rolled[(u - 1) % nt]) for u in range(nt)]
            for u in range(nt):
                mirror = sfull[u, 24 - o, pl.ds(at + a, 8), :]
                symp[u, o, here, :] = (own[u] + mirror) * masks[b][u]

    def sym_body(t, carry):
        sym_tile(pl.multiple_of(OFF + 8 * t, 8), True)
        return carry
    lax.fori_loop(0, nrow // 8, sym_body, 0)

    def sym_halo_body(t, carry):
        sym_tile(pl.multiple_of(OFF - HALO + t * (nrow + HALO), 8), False)
        return carry
    lax.fori_loop(0, 2, sym_halo_body, 0)

    def lap_body(t, carry):
        at = OFF - HALO + 8 * t
        here = pl.ds(pl.multiple_of(at, 8), 8)
        above, below = pl.ds(at - 1, 8), pl.ds(at + 1, 8)
        tiles = lambda k, rows: [cbuf[k, u, rows, :] for u in range(nt)]
        kap, con, inv, msk = (tiles(k, here) for k in range(4))
        con_n = ring_shifts(con, 1, lane)
        east = [0.5 * (con[u] + con_n[u]) for u in range(nt)]
        west = ring_shifts(east, -1, lane)
        inv_e, inv_w = ring_shifts(inv, 1, lane), ring_shifts(inv, -1, lane)
        msk_e, msk_w = ring_shifts(msk, 1, lane), ring_shifts(msk, -1, lane)
        for u in range(nt):
            north = 0.5 * (con[u] + cbuf[1, u, above, :])
            south = 0.5 * (con[u] + cbuf[1, u, below, :])
            diag = kap[u] + north + south + west[u] + east[u]
            lap[0, u, here, :] = inv[u] * diag * msk[u]
            lap[1, u, here, :] = inv[u] * north * cbuf[3, u, above, :]
            lap[2, u, here, :] = inv[u] * south * cbuf[3, u, below, :]
            lap[3, u, here, :] = inv_w[u] * west[u] * msk[u]
            lap[4, u, here, :] = inv_e[u] * east[u] * msk[u]
            lap[5, u, here, :] = msk[u] * diag
            lap[6, u, here, :] = msk[u] * north
            lap[7, u, here, :] = msk[u] * south
            lap[8, u, here, :] = msk_w[u] * west[u]
            lap[9, u, here, :] = msk_e[u] * east[u]
            lap[10, u, here, :] = 1.0 - msk[u]
            if u < nu:
                lap[11, u, here, :] = 1.0 / inv[u]
        return carry
    lax.fori_loop(0, (nrow + 2 * HALO) // 8, lap_body, 0)

    def apply_m(src, dst, start, count):
        def body(t, carry):
            at = start + 8 * t
            for p0 in range(0, PROBES, 2):
                pair_p = (p0, p0 + 1)
                field = {(p, a, u): src[u, p, pl.ds(at + a, 8), :] for p in pair_p for a in range(-2, 3) for u in range(nt)}
                total = {}
                for b in range(-2, 3):
                    part = {}
                    for a in range(-2, 3):
                        o = (a + 2) * 5 + b + 2
                        for u in range(nt):
                            weight = symp[u, o, pl.ds(at, 8), :]
                            for p in pair_p:
                                term = weight * field[p, a, u]
                                part[p, u] = term if a == -2 else part[p, u] + term
                    for p in pair_p:
                        moved = ring_shifts([part[p, u] for u in range(nt)], b, lane)
                        for u in range(nt):
                            total[p, u] = moved[u] if b == -2 else total[p, u] + moved[u]
                for p in pair_p:
                    for u in range(nt):
                        dst[u, p, pl.ds(at, 8), :] = total[p, u]
            return carry
        lax.fori_loop(0, count, body, 0)

    def half_laplace(first, src, at, p, coefs):
        centre = [src[u, p, pl.ds(at, 8), :] for u in range(nt)]
        to_east = ring_shifts([coefs[3][u] * centre[u] for u in range(nt)], 1, lane)
        to_west = ring_shifts([coefs[4][u] * centre[u] for u in range(nt)], -1, lane)
        out = []
        for u in range(nt):
            across = to_east[u] + to_west[u]
            along = coefs[1][u] * src[u, p, pl.ds(at - 1, 8), :] + coefs[2][u] * src[u, p, pl.ds(at + 1, 8), :]
            out.append(coefs[0][u] * centre[u] - (across + along))
        return out

    def inner_a(src, start, count):
        def body(t, carry):
            at = start + 8 * t
            coefs = [[lap[k, u, pl.ds(at, 8), :] for u in range(nt)] for k in range(5)]
            for p in range(PROBES):
                out = half_laplace(0, src, at, p, coefs)
                for u in range(nt):
                    tbuf[u, p, pl.ds(at, 8), :] = out[u]
            return carry
        lax.fori_loop(0, count, body, 0)

    def outer_a(src, dst, start, count, keep):
        def body(t, carry):
            at = start + 8 * t
            coefs = [[lap[5 + k, u, pl.ds(at, 8), :] for u in range(nt)] for k in range(6)]
            for p in range(PROBES):
                out = half_laplace(5, tbuf, at, p, coefs)
                for u in range(keep):
                    dst[u, p, pl.ds(at, 8), :] = out[u] + coefs[5][u] * src[u, p, pl.ds(at, 8), :]
            return carry
        lax.fori_loop(0, count, body, 0)

    pairs = [(k, l) for k in range(8) for l in range(k, 8)]

    groups = -(-len(pairs) // 8)

    def gram(terms):
        def body(i, acc):
            u = i // (nrow // 8)
            rows = pl.ds(pl.multiple_of(OFF + 8 * (i % (nrow // 8)), 8), 8)
            for first, second, weight in terms:
                a = [first[u, p, rows, :] for p in range(PROBES)]
                if weight is not None:
                    w = lap[weight, u, rows, :]
                    a = [w * x for x in a]
                b = [second[u, p, rows, :] for p in range(PROBES)]
                acc = tuple(acc[n] + a[k] * b[l] for n, (k, l) in enumerate(pairs))
            return acc
        start = tuple(jnp.zeros((8, LANES), jnp.float32) for _ in pairs)
        return lax.fori_loop(0, nu * (nrow // 8), body, start)

    def to_lanes(total, first, acc):
        for j in range(groups):
            stacked = None
            for s in range(8):
                if 8 * j + s < len(acc):
                    entry = jnp.broadcast_to(jnp.sum(acc[8 * j + s], axis=0, keepdims=True), (8, LANES))
                    stacked = entry if stacked is None else jnp.where(sub == s, entry, stacked)
            total = jnp.where(lane == first + j, jnp.sum(stacked, axis=1, keepdims=True), total)
        return total

    def one_row(total):
        spread = pltpu.roll(total, 0, axis=1, stride=16, stride_axis=0)
        return jnp.sum(spread, axis=0, keepdims=True)

    def entries(line, first):
        out = [[None] * 8 for _ in range(8)]
        for n, (k, l) in enumerate(pairs):
            at = 16 * (n % 8) + first + n // 8
            out[k][l] = out[l][k] = jnp.broadcast_to(line[:, at : at + 1], (8, LANES))
        return out

    def entry_rows(spread):
        out = []
        for k in range(8):
            line = spread[k][0]
            for l in range(1, 8):
                line = jnp.where(lane == l, spread[k][l], line)
            out.append(line)
        return out

    def post(step, phase, value):
        mine, partners, count = ((mine1, partners1, group1), (pair, partners2, group2))[phase]
        buf = grams.at[step, phase]
        buf[mine] = value
        copies = [pltpu.make_async_remote_copy(
            src_ref=buf.at[mine], dst_ref=buf.at[mine],
            send_sem=gsend.at[step, phase, d], recv_sem=grecv.at[step, phase, mine],
            device_id=who, device_id_type=MESH) for d, who in enumerate(partners)]
        for copy in copies:
            copy.start()

        def finish():
            for d in range(1, count):
                slot = (mine + d) % count
                pltpu.make_async_copy(buf.at[slot], buf.at[slot], grecv.at[step, phase, slot]).wait()
            terms = [buf[k] for k in range(count)]
            while len(terms) > 1:
                terms = [terms[i] + terms[i + 1] for i in range(0, len(terms) - 1, 2)] + terms[len(terms) & ~1 :]
            pending.extend(copies)
            return terms[0]
        return finish

    pending = []
    zeros = jnp.zeros((8, LANES), jnp.float32)

    apply_m(rbuf, zbuf, OFF - 8, (nrow + 16) // 8)
    inner_a(zbuf, OFF - 8, (nrow + 16) // 8)
    outer_a(zbuf, wbuf, OFF - 4, (nrow + 8) // 8, nt)
    total = to_lanes(zeros, 0, gram([(rbuf, zbuf, None)]))
    total = to_lanes(total, groups, gram([(zbuf, wbuf, None)]))
    step0 = post(0, 0, one_row(total))
    apply_m(wbuf, ybuf, OFF - 2, (nrow + 8) // 8)
    step1 = post(1, 0, one_row(to_lanes(zeros, 0, gram([(wbuf, ybuf, None)]))))
    step0 = post(0, 1, step0())
    inner_a(ybuf, OFF - 1, (nrow + 8) // 8)
    step2 = post(2, 0, one_row(to_lanes(zeros, 0, gram([(tbuf, tbuf, 11), (ybuf, ybuf, 10)]))))

    outer_a(ybuf, vbuf, OFF, nrow // 8, nu)
    add = lambda x, y: [a + b for a, b in zip(x, y)]
    minus = lambda x, y: [a - b for a, b in zip(x, y)]

    def keep_coef(m, rows):
        spread = splats(stack_rows(rows, sub), 0)
        for k in range(8):
            for l in range(8):
                coef[m, l, k] = spread[k][l]
        return spread

    def mix(jobs, l0, at_t, u, rows, cols):
        for field, m, base, sign, target in jobs:
            f = [field(k, u, rows, cols) for k in range(8)]
            for l in (l0, l0 + 1):
                total = coef[m, l, 0] * f[0]
                for k in range(1, 8):
                    total = total + coef[m, l, k] * f[k]
                if base is not None:
                    old = base(l, u, rows, cols)
                    total = old + total if sign > 0 else old - total
                elif sign < 0:
                    total = -total
                target[l, at_t, cols] = total

    ext = lambda ref: lambda k, u, rows, cols: ref[u, k, pl.ds(pl.multiple_of(rows + OFF, 8), 8), :]
    flat = lambda ref: lambda k, u, rows, cols: ref[k, pl.ds(pl.multiple_of(rows, 8), 8), cols]

    def mix_all(jobs, l0):
        def body(t, carry):
            for u in range(nu):
                mix(jobs, l0, pl.ds(pl.multiple_of(8 * t, 8), 8), u, 8 * t, slice(u * LANES, (u + 1) * LANES))
            return carry
        lax.fori_loop(0, nrow // 8, body, 0)

    step1 = post(1, 1, step1())
    line0 = step0()
    g1s, g2s = entries(line0, 0), entries(line0, groups)
    g1r, g2r = entry_rows(g1s), entry_rows(g2s)
    alpha = substitute(factor(g2s), g1r)
    alpha_s = keep_coef(0, alpha)
    step2 = post(2, 1, step2())
    for l0 in range(0, PROBES, 2):
        mix_all([(ext(zbuf), 0, None, 1, xs), (ext(wbuf), 0, ext(rbuf), -1, rs),
                 (ext(ybuf), 0, None, -1, ps), (ext(vbuf), 0, None, -1, ws)], l0)
    fact1 = factor(g1s)
    g3s = entries(step1(), 0)
    g3_alpha = product(g3s, alpha)
    gamma = minus(minus(g1r, product(g2s, alpha)), product_t(alpha_s, minus(g2r, g3_alpha)))
    beta = substitute(fact1, gamma)
    eye = [jnp.where(lane == k, 1.0, 0.0) for k in range(8)]
    b_rows = add(beta, eye)
    b_s = keep_coef(1, b_rows)
    part = product_t(b_s, minus(product(g2s, b_rows), g3_alpha))
    g3_b = product(g3s, b_rows)
    for l0 in range(0, PROBES, 2):
        mix_all([(ext(zbuf), 1, flat(ps), 1, ps), (ext(wbuf), 1, flat(ws), 1, ws)], l0)

    g4s = entries(step2(), 0)
    curv = minus(part, product_t(alpha_s, minus(g3_b, product(g4s, alpha))))
    curv_s = splats(stack_rows(curv, sub), 0)
    curv_s = [[0.5 * (curv_s[k][l] + curv_s[l][k]) for l in range(8)] for k in range(8)]
    keep_coef(2, substitute(factor(curv_s), gamma))

    outs = []
    for l in range(PROBES):
        outs.append(pltpu.make_async_copy(xs.at[l], x_out.at[l], osem.at[l]))
        outs.append(pltpu.make_async_copy(rs.at[l], r_out.at[l], osem.at[8 + l]))
    for l0 in range(0, PROBES, 2):
        mix_all([(flat(ps), 2, flat(xs), 1, xs), (flat(ws), 2, flat(rs), -1, rs)], l0)
        for copy in outs[2 * l0 : 2 * l0 + 4]:
            copy.start()
    for copy in pending + col_copies + row_copies:
        copy.wait_send()
    for copy in outs:
        copy.wait()


def shards(probes, kappa_sq, conduct, inv_mass, spai, sea_mask):
    _, nrow, ncol = probes.shape
    rows_n, cols_n = lax.axis_size("row"), lax.axis_size("col")
    nu = ncol // LANES
    nt = nu + 1
    ext = nrow + 2 * OFF
    most = max(2 * cols_n, rows_n // 2)
    f32, bf16 = jnp.float32, jnp.bfloat16
    field = pltpu.VMEM((nt, PROBES, ext, LANES), f32)
    dma = pltpu.SemaphoreType.DMA
    scratch = [
        field, field, field, field, field,
        pltpu.VMEM((25, nrow, ncol), bf16),
        pltpu.VMEM((nt, 25, ext, LANES), f32),
        pltpu.VMEM((nt, 25, ext, LANES), f32),
        pltpu.VMEM((4, nt, ext, LANES), f32),
        pltpu.VMEM((12, nt, ext, LANES), f32),
        pltpu.VMEM((2, 12, HALO, ncol), f32),
        pltpu.VMEM((2, 13, 2 * HALO, ncol), bf16),
        pltpu.VMEM((2, 12, HALO, ncol), f32),
        pltpu.VMEM((2, 13, 2 * HALO, ncol), bf16),
        pltpu.VMEM((nrow, ncol), jnp.int32),
        pltpu.VMEM((2, nrow, LANES), f32),
        pltpu.VMEM((2, nrow, 2 * LANES), bf16),
        pltpu.VMEM((2, nrow + 2 * HALO, LANES), f32),
        pltpu.VMEM((2, ext, 2 * LANES), bf16),
        pltpu.VMEM((3, 2, most, 1, LANES), f32),
        pltpu.VMEM((3, 8, 8, 8, LANES), f32),
        pltpu.VMEM((PROBES, nrow, ncol), f32),
        pltpu.VMEM((PROBES, nrow, ncol), f32),
        pltpu.VMEM((PROBES, nrow, ncol), f32),
        pltpu.VMEM((PROBES, nrow, ncol), f32),
        field,
        dma((2 + 4 * nu,)),
        dma((16,)), dma((16,)),
        dma((3, 2, most)), dma((3, 2, most)),
        dma((16,)),
    ]
    out = jax.ShapeDtypeStruct(probes.shape, f32)
    return pl.pallas_call(
        functools.partial(kernel, nrow, ncol, rows_n, cols_n),
        out_shape=(out, out),
        in_specs=[pl.BlockSpec(memory_space=pl.ANY)] * 6,
        out_specs=(pl.BlockSpec(memory_space=pl.ANY),) * 2,
        scratch_shapes=scratch,
        compiler_params=pltpu.CompilerParams(
            collective_id=0, has_side_effects=True, vmem_limit_bytes=60 * 1024 * 1024),
    )(probes, kappa_sq, conduct, inv_mass, spai, sea_mask)


def solution(mesh):
    field = P(None, "row", "col")
    cell = P("row", "col")
    return jax.shard_map(
        shards, mesh=mesh, in_specs=(field, cell, cell, cell, field, cell),
        out_specs=(field, field), check_vma=False)
```

time: 58.1 us -> 50.8 us (0.87)
  local copies, waits for them, and re-layouts: 7.12 us -> 2.72 us
  Pallas kernels: 50 us -> 47.3 us
    unnamed x14 -> x4, local copies, waits for them, and re-layouts: 7.12 us -> 2.72 us
    pallas_call x1, Pallas kernels: 50 us -> 47.3 us  [shards(): pl.pallas_call(functools.partial(kernel, nrow, ncol, rows_n, cols_n), out...]
where the time goes in v2:
time: 50.8 us; the launch traced here: 50.7 us
  Pallas kernels  47.3 us (93%)
  local copies, waits for them, and re-layouts  2.72 us (5%)
  between operations  0.65 us (1%)
    pallas_call x1, Pallas kernels, shards(): pl.pallas_call(functools.partial(kernel, nrow, ncol, rows_n, cols_n), out...  47.3 us
    unnamed x4, local copies, waits for them, and re-layouts  2.72 us

profile of v2, /device:TPU:1, one launch (start us, length us, event | category | flops | bytes accessed | tf_op | source)
XLA Modules:
  0.0 50.7 jit_solution(2252471377814758163)
XLA Ops:
  0.6 47.3 %shard_map.77 = (f32[8,64,256]{2,1,0:T(8,128)}, f32[8,64,256]{2,1,0:T(8,128)}) custom-call(f32[8,64,256]{2,1,0:T(8,128)} %probes.1, f32[64,256]{1,0:T(8,128)} %kappa.1, f32[64,256]{1,0:T(8,128)} %conduct.1, f32[64,256]{1,0:T(8,128)} %inv_mass.1, bf16[25,64,256]{2,1,0:T(8,128)(2,1)} %spai.1, s32[64,256]{1,0:T(8,128)} %sea.1), custom_call_target="tpu_custom_call" | custom-call | tf_op jit(solution)/shard_map/pallas_call | solution.py:644
  48.0 0.0 copy-start
  48.0 1.9 %copy.10 = f32[8,64,256]{2,1,0:T(8,128)} copy(f32[8,64,256]{2,1,0:T(8,128)} %get-tuple-element.4) | data formatting | bytes 1048576
  49.9 0.0 copy-done
  49.9 0.8 %copy.11 = f32[8,64,256]{2,1,0:T(8,128)} copy(f32[8,64,256]{2,1,0:T(8,128)S(1)} %copy-done) | data formatting | bytes 1048576
Async XLA Ops:
  48.0 1.9 %copy-start = (f32[8,64,256]{2,1,0:T(8,128)S(1)}, f32[8,64,256]{2,1,0:T(8,128)}, u32[]{:S(2)}) copy-start(f32[8,64,256]{2,1,0:T(8,128)} %get-tuple-element.5) | copy-start | bytes 1572868

commit v3 on v2

--- a/solution.py
+++ b/solution.py
@@ -101,11 +101,11 @@
 def kernel(
     nrow, ncol, rows_n, cols_n,
     probes, kappa, conduct, inv_mass, spai, sea,
-    x_out, r_out,
+    xs, rs,
     rbuf, zbuf, wbuf, ybuf, tbuf, sraw, sfull, symp, cbuf, lap,
     fedge, sedge, fland, sland, seaown, cpack, spack, crecv, srecv,
-    grams, coef, xs, rs, ps, ws, vbuf,
-    lsem, ssem, rsem, gsend, grecv, osem,
+    grams, coef, ps, ws, vbuf,
+    lsem, ssem, rsem, gsend, grecv,
 ):
     nu = ncol // LANES
     nt = nu + 1
@@ -184,6 +184,44 @@
     lax.fori_loop(0, nrow // 8, pack_body, 0)
 
     local[0].wait()
+
+    for side, at16, skip in ((0, nrow - 16, 8), (1, 0, 0)):
+        for u in range(nu):
+            cols = slice(u * LANES, (u + 1) * LANES)
+            for j in range(13):
+                first = sraw[2 * j, at16 : at16 + 16, cols].astype(jnp.float32)[skip : skip + 8]
+                second = sraw[min(2 * j + 1, 24), at16 : at16 + 16, cols].astype(jnp.float32)[skip : skip + 8]
+                sedge[side, j, :, cols] = jnp.concatenate([first, second], axis=0).astype(jnp.bfloat16)
+
+    pl.semaphore_wait(barrier, len(around) + len(partners1) + len(partners2))
+
+    def remote(index, src, dst, who):
+        return pltpu.make_async_remote_copy(
+            src_ref=src, dst_ref=dst, send_sem=ssem.at[index], recv_sem=rsem.at[index],
+            device_id=who, device_id_type=MESH)
+
+    row_copies = []
+    for side, who in ((0, down), (1, up)):
+        row_copies.append(remote(2 * side, sedge.at[side], sland.at[side], (who, col)))
+        row_copies.append(remote(2 * side + 1, fedge.at[side], fland.at[side], (who, col)))
+    col_copies = []
+    for side, who in ((0, left), (1, right)):
+        to = 1 - side
+        base = 4 + 6 * side
+        col_copies += [
+            remote(base, spack.at[side, pl.ds(0, OFF), :], srecv.at[to, pl.ds(OFF + nrow, OFF), :], (up, who)),
+            remote(base + 1, cpack.at[side, pl.ds(0, HALO), :], crecv.at[to, pl.ds(HALO + nrow, HALO), :], (up, who)),
+            remote(base + 2, spack.at[side, pl.ds(nrow - OFF, OFF), :], srecv.at[to, pl.ds(0, OFF), :], (down, who)),
+            remote(base + 3, cpack.at[side, pl.ds(nrow - HALO, HALO), :], crecv.at[to, pl.ds(0, HALO), :], (down, who)),
+            remote(base + 4, spack.at[side], srecv.at[to, pl.ds(OFF, nrow), :], (row, who)),
+            remote(base + 5, cpack.at[side], crecv.at[to, pl.ds(HALO, nrow), :], (row, who)),
+        ]
+    for copy in row_copies:
+        copy.start()
+    direct = [copy for k, copy in enumerate(col_copies) if k % 6 >= 4]
+    corners = [copy for k, copy in enumerate(col_copies) if k % 6 < 4]
+    for copy in direct[1::2] + corners[1::2]:
+        copy.start()
 
     def spack_body(t, carry):
         src = pl.ds(pl.multiple_of(16 * t, 16), 16)
@@ -208,38 +246,7 @@
         return carry
     lax.fori_loop(0, nrow // 16, spack_body, 0)
 
-    for side, at in ((0, OFF + nrow - HALO), (1, OFF)):
-        for u in range(nu):
-            cols = slice(u * LANES, (u + 1) * LANES)
-            for j in range(13):
-                first = sfull[u, 2 * j, at : at + 8, :]
-                second = sfull[u, min(2 * j + 1, 24), at : at + 8, :]
-                sedge[side, j, :, cols] = jnp.concatenate([first, second], axis=0).astype(jnp.bfloat16)
-
-    pl.semaphore_wait(barrier, len(around) + len(partners1) + len(partners2))
-
-    def remote(index, src, dst, who):
-        return pltpu.make_async_remote_copy(
-            src_ref=src, dst_ref=dst, send_sem=ssem.at[index], recv_sem=rsem.at[index],
-            device_id=who, device_id_type=MESH)
-
-    row_copies = []
-    for side, who in ((0, down), (1, up)):
-        row_copies.append(remote(2 * side, sedge.at[side], sland.at[side], (who, col)))
-        row_copies.append(remote(2 * side + 1, fedge.at[side], fland.at[side], (who, col)))
-    col_copies = []
-    for side, who in ((0, left), (1, right)):
-        to = 1 - side
-        base = 4 + 6 * side
-        col_copies += [
-            remote(base, spack.at[side, pl.ds(0, OFF), :], srecv.at[to, pl.ds(OFF + nrow, OFF), :], (up, who)),
-            remote(base + 1, cpack.at[side, pl.ds(0, HALO), :], crecv.at[to, pl.ds(HALO + nrow, HALO), :], (up, who)),
-            remote(base + 2, spack.at[side, pl.ds(nrow - OFF, OFF), :], srecv.at[to, pl.ds(0, OFF), :], (down, who)),
-            remote(base + 3, cpack.at[side, pl.ds(nrow - HALO, HALO), :], crecv.at[to, pl.ds(0, HALO), :], (down, who)),
-            remote(base + 4, spack.at[side], srecv.at[to, pl.ds(OFF, nrow), :], (row, who)),
-            remote(base + 5, cpack.at[side], crecv.at[to, pl.ds(HALO, nrow), :], (row, who)),
-        ]
-    for copy in col_copies + row_copies:
+    for copy in direct[0::2] + corners[0::2]:
         copy.start()
 
     one = jnp.float32(1.0)
@@ -257,26 +264,6 @@
                     symp[u, o, here, :] = pltpu.roll(sfull[u, o, here, :], b % LANES, axis=1)
         return carry
     lax.fori_loop(0, nrow // 8, rotate_body, 0)
-
-    for copy in row_copies:
-        copy.wait_recv()
-    for side, keep, at in ((0, has_up, OFF - HALO), (1, has_down, OFF + nrow)):
-        for u in range(nu):
-            cols = slice(u * LANES, (u + 1) * LANES)
-            for k in range(12):
-                item = fland[side, k, :, cols] * keep
-                if k < 8:
-                    rbuf[u, k, at : at + 8, :] = item
-                else:
-                    cbuf[k - 8, u, at : at + 8, :] = item
-            for j in range(13):
-                both = sland[side, j, :, cols].astype(jnp.float32) * keep
-                sfull[u, 2 * j, at : at + 8, :] = both[0:8]
-                if j < 12:
-                    sfull[u, 2 * j + 1, at : at + 8, :] = both[8:16]
-
-    for copy in col_copies:
-        copy.wait_recv()
 
     def inside_rows(first, sublane):
         at = first + sublane
@@ -299,7 +286,6 @@
             else:
                 cbuf[k - 8, nu, dst, :] = tile
         return carry
-    lax.fori_loop(0, (nrow + 2 * HALO) // 8, unpack_body, 0)
 
     def sunpack_body(t, carry):
         src = pl.ds(pl.multiple_of(16 * t, 16), 16)
@@ -314,7 +300,6 @@
                 moved = pltpu.roll(merged[k % 2], (-HALO * k) % LANES, axis=1) if k else merged[0]
                 sfull[nu, 16 * part + k, src, :] = jnp.where(edge_lanes16, moved, 0.0)
         return carry
-    lax.fori_loop(0, (nrow + 2 * OFF) // 16, sunpack_body, 0)
 
     colmask = [jnp.ones((8, LANES), jnp.float32)] * nu + [
         jnp.where(lane < LANES // 2, has_right, has_left)]
@@ -338,19 +323,20 @@
                 mirror = sfull[u, 24 - o, pl.ds(at + a, 8), :]
                 symp[u, o, here, :] = (own[u] + mirror) * masks[b][u]
 
-    def sym_body(t, carry):
-        sym_tile(pl.multiple_of(OFF + 8 * t, 8), True)
-        return carry
-    lax.fori_loop(0, nrow // 8, sym_body, 0)
-
-    def sym_halo_body(t, carry):
-        sym_tile(pl.multiple_of(OFF - HALO + t * (nrow + HALO), 8), False)
-        return carry
-    lax.fori_loop(0, 2, sym_halo_body, 0)
-
-    def lap_body(t, carry):
-        at = OFF - HALO + 8 * t
-        here = pl.ds(pl.multiple_of(at, 8), 8)
+    inner_tiles = nrow // 8 - 2
+    inner_at = lambda t: pl.multiple_of(OFF + 8 + 8 * t, 8)
+    rim_at = lambda t: pl.multiple_of(OFF - HALO + 8 * t + (t // 2) * 8 * inner_tiles, 8)
+    edge_at = lambda t: pl.multiple_of(OFF + t * (nrow - 8), 8)
+    halo_at = lambda t: pl.multiple_of(OFF - HALO + t * (nrow + HALO), 8)
+
+    def each(count, place, body):
+        def step(t, carry):
+            body(place(t))
+            return carry
+        lax.fori_loop(0, count, step, 0)
+
+    def lap_tile(at):
+        here = pl.ds(at, 8)
         above, below = pl.ds(at - 1, 8), pl.ds(at + 1, 8)
         tiles = lambda k, rows: [cbuf[k, u, rows, :] for u in range(nt)]
         kap, con, inv, msk = (tiles(k, here) for k in range(4))
@@ -376,12 +362,9 @@
             lap[10, u, here, :] = 1.0 - msk[u]
             if u < nu:
                 lap[11, u, here, :] = 1.0 / inv[u]
-        return carry
-    lax.fori_loop(0, (nrow + 2 * HALO) // 8, lap_body, 0)
-
-    def apply_m(src, dst, start, count):
-        def body(t, carry):
-            at = start + 8 * t
+
+    def apply_m(src, dst, place, count):
+        def body(at):
             for p0 in range(0, PROBES, 2):
                 pair_p = (p0, p0 + 1)
                 field = {(p, a, u): src[u, p, pl.ds(at + a, 8), :] for p in pair_p for a in range(-2, 3) for u in range(nt)}
@@ -402,8 +385,7 @@
                 for p in pair_p:
                     for u in range(nt):
                         dst[u, p, pl.ds(at, 8), :] = total[p, u]
-            return carry
-        lax.fori_loop(0, count, body, 0)
+        each(count, place, body)
 
     def half_laplace(first, src, at, p, coefs):
         centre = [src[u, p, pl.ds(at, 8), :] for u in range(nt)]
@@ -512,13 +494,44 @@
     pending = []
     zeros = jnp.zeros((8, LANES), jnp.float32)
 
-    apply_m(rbuf, zbuf, OFF - 8, (nrow + 16) // 8)
+    for copy in direct:
+        copy.wait_recv()
+    lax.fori_loop(1, nrow // 8 + 1, unpack_body, 0)
+    each(inner_tiles, inner_at, lap_tile)
+    lax.fori_loop(1, nrow // 16 + 1, sunpack_body, 0)
+    each(inner_tiles, inner_at, lambda at: sym_tile(at, True))
+    apply_m(rbuf, zbuf, inner_at, inner_tiles)
+    for copy in row_copies:
+        copy.wait_recv()
+    for side, keep, at in ((0, has_up, OFF - HALO), (1, has_down, OFF + nrow)):
+        for u in range(nu):
+            cols = slice(u * LANES, (u + 1) * LANES)
+            for k in range(12):
+                item = fland[side, k, :, cols] * keep
+                if k < 8:
+                    rbuf[u, k, at : at + 8, :] = item
+                else:
+                    cbuf[k - 8, u, at : at + 8, :] = item
+            for j in range(13):
+                both = sland[side, j, :, cols].astype(jnp.float32) * keep
+                sfull[u, 2 * j, at : at + 8, :] = both[0:8]
+                if j < 12:
+                    sfull[u, 2 * j + 1, at : at + 8, :] = both[8:16]
+
+    for copy in corners:
+        copy.wait_recv()
+    lax.fori_loop(0, 2, lambda t, carry: unpack_body(t * (nrow // 8 + 1), carry), 0)
+    lax.fori_loop(0, 2, lambda t, carry: sunpack_body(t * (nrow // 16 + 1), carry), 0)
+    each(4, rim_at, lap_tile)
+    each(2, edge_at, lambda at: sym_tile(at, True))
+    each(2, halo_at, lambda at: sym_tile(at, False))
+    apply_m(rbuf, zbuf, rim_at, 4)
     inner_a(zbuf, OFF - 8, (nrow + 16) // 8)
     outer_a(zbuf, wbuf, OFF - 4, (nrow + 8) // 8, nt)
     total = to_lanes(zeros, 0, gram([(rbuf, zbuf, None)]))
     total = to_lanes(total, groups, gram([(zbuf, wbuf, None)]))
     step0 = post(0, 0, one_row(total))
-    apply_m(wbuf, ybuf, OFF - 2, (nrow + 8) // 8)
+    apply_m(wbuf, ybuf, lambda t: OFF - 2 + 8 * t, (nrow + 8) // 8)
     step1 = post(1, 0, one_row(to_lanes(zeros, 0, gram([(wbuf, ybuf, None)]))))
     step0 = post(0, 1, step0())
     inner_a(ybuf, OFF - 1, (nrow + 8) // 8)
@@ -588,17 +601,21 @@
     curv_s = [[0.5 * (curv_s[k][l] + curv_s[l][k]) for l in range(8)] for k in range(8)]
     keep_coef(2, substitute(factor(curv_s), gamma))
 
-    outs = []
-    for l in range(PROBES):
-        outs.append(pltpu.make_async_copy(xs.at[l], x_out.at[l], osem.at[l]))
-        outs.append(pltpu.make_async_copy(rs.at[l], r_out.at[l], osem.at[8 + l]))
     for l0 in range(0, PROBES, 2):
         mix_all([(flat(ps), 2, flat(xs), 1, xs), (flat(ws), 2, flat(rs), -1, rs)], l0)
-        for copy in outs[2 * l0 : 2 * l0 + 4]:
-            copy.start()
     for copy in pending + col_copies + row_copies:
         copy.wait_send()
-    for copy in outs:
+
+
+def copy_kernel(x_in, r_in, x_out, r_out, sem):
+    copies = []
+    for p in range(0, PROBES, 2):
+        two = pl.ds(p, 2)
+        copies.append(pltpu.make_async_copy(x_in.at[two], x_out.at[two], sem.at[p]))
+        copies.append(pltpu.make_async_copy(r_in.at[two], r_out.at[two], sem.at[p + 1]))
+    for copy in copies:
+        copy.start()
+    for copy in copies:
         copy.wait()
 
 
@@ -632,24 +649,30 @@
         pltpu.VMEM((3, 8, 8, 8, LANES), f32),
         pltpu.VMEM((PROBES, nrow, ncol), f32),
         pltpu.VMEM((PROBES, nrow, ncol), f32),
-        pltpu.VMEM((PROBES, nrow, ncol), f32),
-        pltpu.VMEM((PROBES, nrow, ncol), f32),
         field,
         dma((2 + 4 * nu,)),
         dma((16,)), dma((16,)),
         dma((3, 2, most)), dma((3, 2, most)),
-        dma((16,)),
     ]
     out = jax.ShapeDtypeStruct(probes.shape, f32)
-    return pl.pallas_call(
+    hbm = pl.BlockSpec(memory_space=pl.ANY)
+    parts = pl.pallas_call(
         functools.partial(kernel, nrow, ncol, rows_n, cols_n),
-        out_shape=(out, out),
-        in_specs=[pl.BlockSpec(memory_space=pl.ANY)] * 6,
-        out_specs=(pl.BlockSpec(memory_space=pl.ANY),) * 2,
+        out_shape=(pltpu.VMEM(probes.shape, f32),) * 2,
+        in_specs=[pl.BlockSpec(memory_space=pltpu.HBM)] * 6,
+        out_specs=(pl.BlockSpec(memory_space=pltpu.VMEM),) * 2,
         scratch_shapes=scratch,
         compiler_params=pltpu.CompilerParams(
-            collective_id=0, has_side_effects=True, vmem_limit_bytes=60 * 1024 * 1024),
-    )(probes, kappa_sq, conduct, inv_mass, spai, sea_mask)
+            collective_id=0, has_side_effects=True, vmem_limit_bytes=48 * 1024 * 1024),
+    )(*[pltpu.with_memory_space_constraint(v, pltpu.HBM) for v in (probes, kappa_sq, conduct, inv_mass, spai, sea_mask)])
+    return pl.pallas_call(
+        copy_kernel,
+        out_shape=(out, out),
+        in_specs=[hbm] * 2,
+        out_specs=(pl.BlockSpec(memory_space=pltpu.HBM),) * 2,
+        scratch_shapes=[dma((8,))],
+        compiler_params=pltpu.CompilerParams(vmem_limit_bytes=16 * 1024 * 1024),
+    )(*parts)
 
 
 def solution(mesh):

time: 50.8 us -> 46.2 us (0.909)
  local copies, waits for them, and re-layouts: 2.72 us -> 0 us
  Pallas kernels: 47.3 us -> 45.5 us
    pallas_call x1, Pallas kernels: 47.3 us -> 44.4 us  [shards(): pl.pallas_call(functools.partial(kernel, nrow, ncol, rows_n, cols_n), out...]
    unnamed x4 -> x0, local copies, waits for them, and re-layouts: 2.72 us -> none
    pallas_call x0 -> x1, Pallas kernels: none -> 1.03 us  [shards(): pl.pallas_call(copy_kernel, out_shape=(out, out), in_specs=[hbm] * 2, out...]
where the time goes in v3:
time: 46.2 us; the launch traced here: 46.1 us
  Pallas kernels  45.5 us (98%)
  between operations  0.64 us (1%)
    pallas_call x1, Pallas kernels, shards(): pl.pallas_call(functools.partial(kernel, nrow, ncol, rows_n, cols_n), out...  44.4 us
    pallas_call x1, Pallas kernels, shards(): pl.pallas_call(copy_kernel, out_shape=(out, out), in_specs=[hbm] * 2, out...  1.03 us

profile of v3, /device:TPU:1, one launch (start us, length us, event | category | flops | bytes accessed | tf_op | source)
XLA Modules:
  0.0 46.1 jit_solution(9532042052382676137)
XLA Ops:
  0.6 44.4 %shard_map.77 = (f32[8,64,256]{2,1,0:T(8,128)S(1)}, f32[8,64,256]{2,1,0:T(8,128)S(1)}) custom-call(f32[8,64,256]{2,1,0:T(8,128)} %probes.1, f32[64,256]{1,0:T(8,128)} %kappa.1, f32[64,256]{1,0:T(8,128)} %conduct.1, f32[64,256]{1,0:T(8,128)} %inv_mass.1, bf16[25,64,256]{2,1,0:T(8,128)(2,1)} %spai.1, s32[64,256]{1,0:T(8,128)} %sea.1), custom_call_target="tpu_custom_call" | custom-call | tf_op jit(solution)/shard_map/pallas_call | solution.py:659
  45.1 1.0 %shard_map.78 = (f32[8,64,256]{2,1,0:T(8,128)}, f32[8,64,256]{2,1,0:T(8,128)}) custom-call(f32[8,64,256]{2,1,0:T(8,128)S(1)} %get-tuple-element.4.x_in, f32[8,64,256]{2,1,0:T(8,128)S(1)} %get-tuple-element.5.r_in), custom_call_target="tpu_custom_call" | custom-call | tf_op jit(solution)/shard_map/pallas_call | solution.py:668

commit v4 on v3

--- a/solution.py
+++ b/solution.py
@@ -437,7 +437,7 @@
                 acc = tuple(acc[n] + a[k] * b[l] for n, (k, l) in enumerate(pairs))
             return acc
         start = tuple(jnp.zeros((8, LANES), jnp.float32) for _ in pairs)
-        return lax.fori_loop(0, nu * (nrow // 8), body, start)
+        return lax.fori_loop(0, nu * (nrow // 8), body, start, unroll=2)
 
     def to_lanes(total, first, acc):
         for j in range(groups):

time: 46.2 us -> 45.7 us (0.989)
  Pallas kernels: 45.5 us -> 45 us
where the time goes in v4:
time: 45.7 us; the launch traced here: 45.6 us
  Pallas kernels  45 us (98%)
  between operations  0.64 us (1%)
    pallas_call x1, Pallas kernels, shards(): pl.pallas_call(functools.partial(kernel, nrow, ncol, rows_n, cols_n), out...  44 us
    pallas_call x1, Pallas kernels, shards(): pl.pallas_call(copy_kernel, out_shape=(out, out), in_specs=[hbm] * 2, out...  1.03 us

profile of v4, /device:TPU:1, one launch (start us, length us, event | category | flops | bytes accessed | tf_op | source)
XLA Modules:
  0.0 45.6 jit_solution(10129830785071964208)
XLA Ops:
  0.6 44.0 %shard_map.77 = (f32[8,64,256]{2,1,0:T(8,128)S(1)}, f32[8,64,256]{2,1,0:T(8,128)S(1)}) custom-call(f32[8,64,256]{2,1,0:T(8,128)} %probes.1, f32[64,256]{1,0:T(8,128)} %kappa.1, f32[64,256]{1,0:T(8,128)} %conduct.1, f32[64,256]{1,0:T(8,128)} %inv_mass.1, bf16[25,64,256]{2,1,0:T(8,128)(2,1)} %spai.1, s32[64,256]{1,0:T(8,128)} %sea.1), custom_call_target="tpu_custom_call" | custom-call | tf_op jit(solution)/shard_map/pallas_call | solution.py:659
  44.6 1.0 %shard_map.78 = (f32[8,64,256]{2,1,0:T(8,128)}, f32[8,64,256]{2,1,0:T(8,128)}) custom-call(f32[8,64,256]{2,1,0:T(8,128)S(1)} %get-tuple-element.4.x_in, f32[8,64,256]{2,1,0:T(8,128)S(1)} %get-tuple-element.5.r_in), custom_call_target="tpu_custom_call" | custom-call | tf_op jit(solution)/shard_map/pallas_call | solution.py:668
